TPU v7x, 32 devices: a whole 2x2x4 slice. The times are simulated.
32 devices in a mesh: dp: 8 (over z, y), seq: 4 (over x, core).
Axes of the slice: x: 2, y: 2, z: 4, core: 2. Of those that a mesh axis runs over, the one named last changes fastest.
Arguments:
- tokens: bfloat16 [8, 1024, 768], P('dp', 'seq'), may hold values from -6 to 6
- conditioning: bfloat16 [8, 768], P('dp'), may hold values from -6 to 6
- cotangent: bfloat16 [8, 1024, 768], P('dp', 'seq'), may hold values from -6 to 6
- ada_weight: bfloat16 [2, 768, 4608], P(None, ('dp', 'seq')), may hold values from -0.21875 to 0.21875
- ada_bias: bfloat16 [2, 4608], P(None, ('dp', 'seq')), may hold values from -3 to 3
- qkv_weight: bfloat16 [2, 768, 2304], P(None, ('dp', 'seq')), may hold values from -0.21875 to 0.21875
- qv_bias: bfloat16 [2, 1536], P(None, ('dp', 'seq')), may hold values from -3 to 3
- proj_weight: bfloat16 [2, 768, 768], P(None, ('dp', 'seq')), may hold values from -0.875 to 0.875
- proj_bias: bfloat16 [2, 768], P(None, ('dp', 'seq')), may hold values from -2 to 2
- fc1_weight: bfloat16 [2, 768, 3072], P(None, ('dp', 'seq')), may hold values from -0.21875 to 0.21875
- fc1_bias: bfloat16 [2, 3072], P(None, ('dp', 'seq')), may hold values from -3 to 3
- fc2_weight: bfloat16 [2, 3072, 768], P(None, ('dp', 'seq')), may hold values from -0.109375 to 0.109375
- fc2_bias: bfloat16 [2, 768], P(None, ('dp', 'seq')), may hold values from -2 to 2
Outputs:
- block_out: float32 [8, 1024, 768], P('dp', 'seq')
- input_grad: float32 [8, 1024, 768], P('dp', 'seq')
- cond_grad: float32 [8, 768], P('dp')
- ada_weight_grad: float32 [2, 768, 4608], P(None, ('dp', 'seq'))
- ada_bias_grad: float32 [2, 4608], P(None, ('dp', 'seq'))
- qkv_weight_grad: float32 [2, 768, 2304], P(None, ('dp', 'seq'))
- qv_bias_grad: float32 [2, 1536], P(None, ('dp', 'seq'))
- proj_weight_grad: float32 [2, 768, 768], P(None, ('dp', 'seq'))
- proj_bias_grad: float32 [2, 768], P(None, ('dp', 'seq'))
- fc1_weight_grad: float32 [2, 768, 3072], P(None, ('dp', 'seq'))
- fc1_bias_grad: float32 [2, 3072], P(None, ('dp', 'seq'))
- fc2_weight_grad: float32 [2, 3072, 768], P(None, ('dp', 'seq'))
- fc2_bias_grad: float32 [2, 768], P(None, ('dp', 'seq'))
All inputs are finite; a program needn't handle non-finite values.
Results may differ from a plain program's by a relative error of at most 0.019.
The roundings to bfloat16 on the way count: a program that leaves them out, or rounds other values in their place, can miss the bound.
Values may be sent and summed in bfloat16 or wider, within the bound.
A program may use at most 320 MiB of HBM per device.

v0:
```python
import jax
import jax.numpy as jnp
from jax import lax
from jax.sharding import PartitionSpec as P

HD = 64


epsilon = 1e-06


def layer_norm(values):
    center = values - jnp.mean(values, axis=-1, keepdims=True)
    spread = jnp.mean(center * center, axis=-1, keepdims=True)
    return center * lax.rsqrt(spread + epsilon)


def norm_back(values, grad):
    return jax.vjp(layer_norm, values)[1](grad)[0]


def gelu_tanh(values):
    return jax.nn.gelu(values, approximate=True)


def gelu_back(values, grad):
    return jax.vjp(gelu_tanh, values)[1](grad)[0]


def project(left, weight):
    return jnp.einsum("btd,de->bte", left, weight, preferred_element_type=jnp.float32)


def project_back(grad, weight):
    return jnp.einsum("bte,de->btd", grad, weight, preferred_element_type=jnp.float32)


def outer_sum(left, grad):
    return jnp.einsum("btd,bte->de", left, grad, preferred_element_type=jnp.float32)


def column_sums(grad):
    return jnp.sum(grad.astype(jnp.float32), axis=(0, 1))


def split_mods(params, cond_low):
    width = params[0].shape[0]
    mods = jnp.dot(cond_low, params[0], preferred_element_type=jnp.float32) + params[1].astype(
        jnp.float32
    )
    return mods.reshape(mods.shape[0], 6, 1, width)


def attention_one(heads):
    length, _, inner = heads.shape
    pieces = heads.reshape(length, 3, inner // HD, HD)
    queries, keys_in, values_in = (pieces[:, 0], pieces[:, 1], pieces[:, 2])
    scores = jnp.einsum(
        "qhe,khe->hqk", queries, keys_in, preferred_element_type=jnp.float32
    ) * HD ** (-0.5)
    row_max = jnp.max(scores, axis=-1, keepdims=True)
    exponent = jnp.exp(scores - row_max)
    row_sum = jnp.sum(exponent, axis=-1, keepdims=True)
    probability = (exponent / row_sum).astype(jnp.bfloat16)
    log_total = row_max + jnp.log(row_sum)
    result = jnp.einsum("hqk,khe->qhe", probability, values_in, preferred_element_type=jnp.float32)
    return (result.astype(jnp.bfloat16).reshape(length, inner), log_total)


def attention(heads):
    return lax.map(attention_one, heads)


def attention_back_one(item):
    heads, log_total, grad_heads = item
    length, _, inner = heads.shape
    pieces = heads.reshape(length, 3, inner // HD, HD)
    queries, keys_in, values_in = (pieces[:, 0], pieces[:, 1], pieces[:, 2])
    grad_out = grad_heads.reshape(length, inner // HD, HD)
    score_scale = HD ** (-0.5)
    scores = (
        jnp.einsum("qhe,khe->hqk", queries, keys_in, preferred_element_type=jnp.float32)
        * score_scale
    )
    probability = jnp.exp(scores - log_total)
    grad_prob = jnp.einsum("qhe,khe->hqk", grad_out, values_in, preferred_element_type=jnp.float32)
    row_dot = jnp.sum(probability * grad_prob, axis=-1, keepdims=True)
    grad_scores = (probability * (grad_prob - row_dot)).astype(jnp.bfloat16)
    grad_q = (
        jnp.einsum("hqk,khe->qhe", grad_scores, keys_in, preferred_element_type=jnp.float32)
        * score_scale
    )
    grad_k = (
        jnp.einsum("hqk,qhe->khe", grad_scores, queries, preferred_element_type=jnp.float32)
        * score_scale
    )
    grad_v = jnp.einsum(
        "hqk,qhe->khe",
        probability.astype(jnp.bfloat16),
        grad_out,
        preferred_element_type=jnp.float32,
    )
    stacked = jnp.stack([grad_q, grad_k, grad_v], axis=1).astype(jnp.bfloat16)
    return stacked.reshape(length, 3, inner)


def attention_back(heads, log_total, grad_heads):
    return lax.map(attention_back_one, (heads, log_total, grad_heads))


def forward_layer(params, resid, cond_low):
    qkv_w, qv_b, proj_w, proj_b, fc1_w, fc1_b, fc2_w, fc2_b = params[2:]
    mods = split_mods(params, cond_low)
    width = resid.shape[2]
    attn_in = (layer_norm(resid) * (1.0 + mods[:, 1]) + mods[:, 0]).astype(jnp.bfloat16)
    query_bias = qv_b[:width].astype(jnp.float32)
    value_bias = qv_b[width:].astype(jnp.float32)
    bias_full = jnp.concatenate([query_bias, jnp.zeros((width,), jnp.float32), value_bias])
    joined = (project(attn_in, qkv_w) + bias_full).astype(jnp.bfloat16)
    joined = joined.reshape(resid.shape[0], resid.shape[1], 3, width)
    heads = lax.all_to_all(joined, "seq", split_axis=3, concat_axis=1, tiled=True)
    attended, log_total = attention(heads)
    attn_tok = lax.all_to_all(attended, "seq", split_axis=1, concat_axis=2, tiled=True)
    branch = project(attn_tok, proj_w) + proj_b.astype(jnp.float32)
    middle = resid + mods[:, 2] * branch
    mlp_in = (layer_norm(middle) * (1.0 + mods[:, 4]) + mods[:, 3]).astype(jnp.bfloat16)
    hidden_pre = project(mlp_in, fc1_w) + fc1_b.astype(jnp.float32)
    hidden_act = gelu_tanh(hidden_pre).astype(jnp.bfloat16)
    mlp_out = project(hidden_act, fc2_w) + fc2_b.astype(jnp.float32)
    result = middle + mods[:, 5] * mlp_out
    kept = (
        resid,
        attn_in,
        heads,
        log_total,
        attn_tok,
        branch,
        middle,
        mlp_in,
        hidden_pre,
        hidden_act,
        mlp_out,
    )
    return (result, kept)


def backward_layer(params, kept, grad_new, cond_low):
    (
        resid,
        attn_in,
        heads,
        log_total,
        attn_tok,
        branch,
        middle,
        mlp_in,
        hidden_pre,
        hidden_act,
        mlp_out,
    ) = kept
    ada_w, ada_b, qkv_w, qv_b, proj_w, proj_b, fc1_w, fc1_b, fc2_w, fc2_b = params
    mods = split_mods(params, cond_low)
    latents, rows, width = resid.shape
    grad_mlp = (grad_new * mods[:, 5]).astype(jnp.bfloat16)
    grad_fc2_w = outer_sum(hidden_act, grad_mlp)
    grad_fc2_b = column_sums(grad_mlp)
    grad_hidden = project_back(grad_mlp, fc2_w)
    grad_pre = gelu_back(hidden_pre, grad_hidden).astype(jnp.bfloat16)
    grad_fc1_w = outer_sum(mlp_in, grad_pre)
    grad_fc1_b = column_sums(grad_pre)
    grad_mlp_in = project_back(grad_pre, fc1_w)
    normed_mid = layer_norm(middle)
    grad_shift_m = jnp.sum(grad_mlp_in, axis=1)
    grad_scale_m = jnp.sum(grad_mlp_in * normed_mid, axis=1)
    grad_gate_m = jnp.sum(grad_new * mlp_out, axis=1)
    grad_middle = grad_new + norm_back(middle, grad_mlp_in * (1.0 + mods[:, 4]))
    grad_gate_a = jnp.sum(grad_middle * branch, axis=1)
    grad_branch = (grad_middle * mods[:, 2]).astype(jnp.bfloat16)
    grad_proj_w = outer_sum(attn_tok, grad_branch)
    grad_proj_b = column_sums(grad_branch)
    grad_attended = project_back(grad_branch, proj_w).astype(jnp.bfloat16)
    grad_heads = lax.all_to_all(grad_attended, "seq", split_axis=2, concat_axis=1, tiled=True)
    grad_joined_heads = attention_back(heads, log_total, grad_heads)
    grad_joined = lax.all_to_all(grad_joined_heads, "seq", split_axis=1, concat_axis=3, tiled=True)
    grad_joined = grad_joined.reshape(latents, rows, 3 * width)
    grad_qkv_w = outer_sum(attn_in, grad_joined)
    joined_sums = column_sums(grad_joined)
    grad_qv_b = jnp.concatenate([joined_sums[:width], joined_sums[2 * width :]])
    grad_attn_in = project_back(grad_joined, qkv_w)
    normed_in = layer_norm(resid)
    grad_shift_a = jnp.sum(grad_attn_in, axis=1)
    grad_scale_a = jnp.sum(grad_attn_in * normed_in, axis=1)
    grad_resid = grad_middle + norm_back(resid, grad_attn_in * (1.0 + mods[:, 1]))
    grad_mods = jnp.stack(
        [grad_shift_a, grad_scale_a, grad_gate_a, grad_shift_m, grad_scale_m, grad_gate_m], axis=1
    )
    grad_mods = grad_mods.reshape(latents, 6 * width)
    grad_mods = lax.psum(grad_mods, "seq").astype(jnp.bfloat16)
    grad_cond = jnp.einsum("bm,dm->bd", grad_mods, ada_w, preferred_element_type=jnp.float32)
    grads = (
        grad_qkv_w,
        grad_qv_b,
        grad_proj_w,
        grad_proj_b,
        grad_fc1_w,
        grad_fc1_b,
        grad_fc2_w,
        grad_fc2_b,
    )
    return (grad_resid, grads, grad_cond, grad_mods)


def on_device(
    tokens,
    conditioning,
    cotangent,
    ada_weight,
    ada_bias,
    qkv_weight,
    qv_bias,
    proj_weight,
    proj_bias,
    fc1_weight,
    fc1_bias,
    fc2_weight,
    fc2_bias,
):
    layers = ada_weight.shape[0]
    cond_f32 = conditioning.astype(jnp.float32)
    cond_low = jax.nn.silu(cond_f32).astype(jnp.bfloat16)
    cond_every = lax.all_gather(cond_low, "dp", axis=0, tiled=True)
    owner = lax.axis_index(("dp", "seq"))
    own_rows = ada_weight.shape[1]
    own_cols = ada_bias.shape[1]
    cond_rows = lax.dynamic_slice_in_dim(cond_every, owner * own_rows, own_rows, 1)
    resid = tokens.astype(jnp.float32)
    kept_all = []
    for layer_at in range(layers):
        params = (
            lax.all_gather(ada_weight[layer_at], ("dp", "seq"), axis=0, tiled=True),
            lax.all_gather(ada_bias[layer_at], ("dp", "seq"), axis=0, tiled=True),
            lax.all_gather(qkv_weight[layer_at], ("dp", "seq"), axis=0, tiled=True),
            lax.all_gather(qv_bias[layer_at], ("dp", "seq"), axis=0, tiled=True),
            lax.all_gather(proj_weight[layer_at], ("dp", "seq"), axis=0, tiled=True),
            lax.all_gather(proj_bias[layer_at], ("dp", "seq"), axis=0, tiled=True),
            lax.all_gather(fc1_weight[layer_at], ("dp", "seq"), axis=0, tiled=True),
            lax.all_gather(fc1_bias[layer_at], ("dp", "seq"), axis=0, tiled=True),
            lax.all_gather(fc2_weight[layer_at], ("dp", "seq"), axis=0, tiled=True),
            lax.all_gather(fc2_bias[layer_at], ("dp", "seq"), axis=0, tiled=True),
        )
        resid, kept = forward_layer(params, resid, cond_low)
        kept_all.append(kept)
    grad_resid = cotangent.astype(jnp.float32)
    grad_cond = jnp.zeros(cond_f32.shape, jnp.float32)
    owned = [None] * layers
    ada_w_out = [None] * layers
    ada_b_out = [None] * layers
    for layer_at in reversed(range(layers)):
        params = (
            lax.all_gather(ada_weight[layer_at], ("dp", "seq"), axis=0, tiled=True),
            lax.all_gather(ada_bias[layer_at], ("dp", "seq"), axis=0, tiled=True),
            lax.all_gather(qkv_weight[layer_at], ("dp", "seq"), axis=0, tiled=True),
            lax.all_gather(qv_bias[layer_at], ("dp", "seq"), axis=0, tiled=True),
            lax.all_gather(proj_weight[layer_at], ("dp", "seq"), axis=0, tiled=True),
            lax.all_gather(proj_bias[layer_at], ("dp", "seq"), axis=0, tiled=True),
            lax.all_gather(fc1_weight[layer_at], ("dp", "seq"), axis=0, tiled=True),
            lax.all_gather(fc1_bias[layer_at], ("dp", "seq"), axis=0, tiled=True),
            lax.all_gather(fc2_weight[layer_at], ("dp", "seq"), axis=0, tiled=True),
            lax.all_gather(fc2_bias[layer_at], ("dp", "seq"), axis=0, tiled=True),
        )
        grad_resid, grads, grad_part, grad_mods = backward_layer(
            params, kept_all[layer_at], grad_resid, cond_low
        )
        grad_cond = grad_cond + grad_part
        mods_every = lax.all_gather(grad_mods, "dp", axis=0, tiled=True)
        ada_w_out[layer_at] = jnp.einsum(
            "bd,bm->dm", cond_rows, mods_every, preferred_element_type=jnp.float32
        )
        mods_total = jnp.sum(mods_every.astype(jnp.float32), axis=0)
        ada_b_out[layer_at] = lax.dynamic_slice_in_dim(mods_total, owner * own_cols, own_cols, 0)
        owned[layer_at] = (
            lax.psum_scatter(grads[0], ("dp", "seq"), scatter_dimension=0, tiled=True),
            lax.psum_scatter(grads[1], ("dp", "seq"), scatter_dimension=0, tiled=True),
            lax.psum_scatter(grads[2], ("dp", "seq"), scatter_dimension=0, tiled=True),
            lax.psum_scatter(grads[3], ("dp", "seq"), scatter_dimension=0, tiled=True),
            lax.psum_scatter(grads[4], ("dp", "seq"), scatter_dimension=0, tiled=True),
            lax.psum_scatter(grads[5], ("dp", "seq"), scatter_dimension=0, tiled=True),
            lax.psum_scatter(grads[6], ("dp", "seq"), scatter_dimension=0, tiled=True),
            lax.psum_scatter(grads[7], ("dp", "seq"), scatter_dimension=0, tiled=True),
        )
    results = [
        jnp.stack([owned[layer_at][member] for layer_at in range(layers)]) for member in range(8)
    ]
    ada_w_grad = jnp.stack(ada_w_out)
    ada_b_grad = jnp.stack(ada_b_out)
    cond_out = jax.vjp(jax.nn.silu, cond_f32)[1](grad_cond)[0]
    return (
        resid,
        grad_resid,
        cond_out,
        ada_w_grad,
        ada_b_grad,
        results[0],
        results[1],
        results[2],
        results[3],
        results[4],
        results[5],
        results[6],
        results[7],
    )


def solution(mesh):
    placed = (
        P("dp", "seq", None),
        P("dp", None),
        P("dp", "seq", None),
        P(None, ("dp", "seq"), None),
        P(None, ("dp", "seq")),
        P(None, ("dp", "seq"), None),
        P(None, ("dp", "seq")),
        P(None, ("dp", "seq"), None),
        P(None, ("dp", "seq")),
        P(None, ("dp", "seq"), None),
        P(None, ("dp", "seq")),
        P(None, ("dp", "seq"), None),
        P(None, ("dp", "seq")),
    )
    return jax.shard_map(
        on_device,
        mesh=mesh,
        in_specs=placed,
        out_specs=(
            P("dp", "seq", None),
            P("dp", "seq", None),
            P("dp", None),
            P(None, ("dp", "seq"), None),
            P(None, ("dp", "seq")),
            P(None, ("dp", "seq"), None),
            P(None, ("dp", "seq")),
            P(None, ("dp", "seq"), None),
            P(None, ("dp", "seq")),
            P(None, ("dp", "seq"), None),
            P(None, ("dp", "seq")),
            P(None, ("dp", "seq"), None),
            P(None, ("dp", "seq")),
        ),
        check_vma=False,
    )
```

profile of v0, /device:TPU:0, one launch (start us, length us, event | category | flops | bytes accessed | tf_op | source)
XLA Modules:
  0.0 1792.7 jit_solution(13910279622905087876)
XLA Ops:
  21.5 43.8 %all-reduce.20 = (bf16[1536]{0:T(1024)(128)(2,1)S(1)}, bf16[4608]{0:T(1024)(128)(2,1)S(1)}, bf16[768]{0:T(1024)(128)(2,1)}, bf16[768]{0:T(1024)(128)(2,1)}, bf16...) all-reduce(bf16[1536]{0:T(1024)(128)(2,1)S(1)} %dynamic-update-slic, ...), channel_id=5, replica_groups=mesh['dp'=8,'seq'=4] {'dp','seq'}, use_global_device_ids=true, to_apply=%add.1 | all-reduce | flops 21504 | bytes 86016
  67.0 20.2 %all-gather.34.cloned.1.call-done = bf16[1,768,4608]{2,1,0:T(8,128)(2,1)} async-done(((bf16[1,24,4608]{2,1,0:T(8,128)(2,1)}), bf16[1,768,4608]{2,1,0:T(8,128)(2,1)}) %all-gather.34.cloned.1.call-update) | async-done | bytes 7077904 | tf_op jit(solution)/shard_map/all_gather | solution.py:240
  87.2 4.0 fusion.94
  91.3 70.3 %all-gather.44.cloned.1.call-done = bf16[1,768,4608]{2,1,0:T(8,128)(2,1)} async-done(((bf16[1,24,4608]{2,1,0:T(8,128)(2,1)}), bf16[1,768,4608]{2,1,0:T(8,128)(2,1)}) %all-gather.44.cloned.1.call-update) | async-done | bytes 7077904 | tf_op jit(solution)/shard_map/all_gather | solution.py:240
  161.6 4.0 fusion.97
  166.9 56.8 %all-gather.36.cloned.1.call-done = bf16[1,768,2304]{2,1,0:T(8,128)(2,1)} async-done(((bf16[1,24,2304]{2,1,0:T(8,128)(2,1)}), bf16[1,768,2304]{2,1,0:T(8,128)(2,1)}) %all-gather.36.cloned.1.call-update) | async-done | bytes 3538960 | tf_op jit(solution)/shard_map/all_gather | solution.py:242
  233.8 20.8 %all-to-all-done = bf16[1,256,3,768]{1,2,0,3:T(4,128)(2,1)S(1)} async-done(((bf16[1,256,3,768]{1,2,0,3:T(4,128)(2,1)}), bf16[1,256,3,768]{1,2,0,3:T(4,128)(2,1)S(1)}, u32[]{:S(2)}, u32[]{:S(2)}) %all-to-all-start) | async-done | bytes 1179680 | tf_op jit(solution)/shard_map/all_to_all | solution.py:121
  267.1 4.0 reduce.82
  278.6 4.9 all-to-all-done.1
  288.4 57.5 %all-gather.40.cloned.1.call-done = bf16[1,768,3072]{2,1,0:T(8,128)(2,1)} async-done(((bf16[1,24,3072]{2,1,0:T(8,128)(2,1)}), bf16[1,768,3072]{2,1,0:T(8,128)(2,1)}) %all-gather.40.cloned.1.call-update) | async-done | bytes 4718608 | tf_op jit(solution)/shard_map/all_gather | solution.py:246
  345.9 5.6 fusion.34
  351.5 60.2 %all-gather.42.cloned.1.call-done = bf16[1,3072,768]{2,1,0:T(8,128)(2,1)} async-done(((bf16[1,96,768]{2,1,0:T(8,128)(2,1)}), bf16[1,3072,768]{2,1,0:T(8,128)(2,1)}) %all-gather.42.cloned.1.call-update) | async-done | bytes 4718608 | tf_op jit(solution)/shard_map/all_gather | solution.py:248
  411.7 6.1 fusion.195
  418.1 55.4 %all-gather.46.cloned.1.call-done = bf16[1,768,2304]{2,1,0:T(8,128)(2,1)} async-done(((bf16[1,24,2304]{2,1,0:T(8,128)(2,1)}), bf16[1,768,2304]{2,1,0:T(8,128)(2,1)}) %all-gather.46.cloned.1.call-update) | async-done | bytes 3538960 | tf_op jit(solution)/shard_map/all_gather | solution.py:242
  473.5 4.2 fusion.41
  482.4 24.0 %all_to_all.120 = bf16[1,256,3,768]{1,2,0,3:T(4,128)(2,1)S(1)} all-to-all(bf16[1,256,3,768]{1,2,0,3:T(4,128)(2,1)S(1)} %copy.120), channel_id=1, replica_groups=mesh['dp'=8,'seq'=4] {'seq'}, dimensions={3} | all-to-all | bytes 2359296 | tf_op jit(solution)/shard_map/all_to_all | solution.py:121
  525.2 4.8 reduce.83
  536.2 6.2 all-to-all-done.3
  551.9 43.6 %all-gather.50.cloned.1.call-done = bf16[1,768,3072]{2,1,0:T(8,128)(2,1)} async-done(((bf16[1,24,3072]{2,1,0:T(8,128)(2,1)}), bf16[1,768,3072]{2,1,0:T(8,128)(2,1)}) %all-gather.50.cloned.1.call-update) | async-done | bytes 4718608 | tf_op jit(solution)/shard_map/all_gather | solution.py:246
  595.6 5.5 fusion.37
  601.1 60.3 %all-gather.52.cloned.1.call-done = bf16[1,3072,768]{2,1,0:T(8,128)(2,1)} async-done(((bf16[1,96,768]{2,1,0:T(8,128)(2,1)}), bf16[1,3072,768]{2,1,0:T(8,128)(2,1)}) %all-gather.52.cloned.1.call-update) | async-done | bytes 4718608 | tf_op jit(solution)/shard_map/all_gather | solution.py:248
  661.4 7.0 convert_reduce_fusion
  681.9 4.7 reduce.84
  688.4 4.3 all-to-all-start.4
  693.5 6.7 all-to-all-done.4
  707.8 7.9 fusion.76
  715.7 8.1 multiply_reduce_fusion.1
  723.8 5.3 multiply_convert_fusion.1
  729.1 5.8 fusion.73
  748.5 6.3 pad_maximum_fusion
  754.8 4.5 all-to-all-start.5
  762.8 22.2 %all-to-all-done.5 = bf16[1,1024,3,192]{3,2,0,1:T(4,128)(2,1)} async-done(((bf16[1,1024,3,192]{3,2,0,1:T(4,128)(2,1)}), bf16[1,1024,3,192]{3,2,0,1:T(4,128)(2,1)}, u32[]{:S(2)}, u32[]{:S(2)}) %all-to-all-start.5) | async-done | bytes 1179680 | tf_op jit(solution)/shard_map/all_to_all | solution.py:184
  785.1 4.3 copy.160
  791.1 4.5 fusion.120
  797.8 3.7 convert_reduce_fusion.1
  809.2 5.4 fusion.185
  820.3 3.7 reduce.85
  825.9 4.1 all-to-all-start.6
  831.0 7.6 all-to-all-done.6
  841.3 6.9 fusion.79
  850.2 6.3 multiply_reduce_fusion
  856.6 6.8 multiply_convert_fusion
  868.0 4.0 fusion.74
  872.8 5.2 pad_maximum_fusion.1
  878.1 29.1 %all_to_all.121 = bf16[1,1024,3,192]{3,2,0,1:T(4,128)(2,1)} all-to-all(bf16[1,1024,3,192]{3,2,0,1:T(4,128)(2,1)S(1)} %pad_maximum_fusion.1), channel_id=1, replica_groups=mesh['dp'=8,'seq'=4] {'seq'}, dimensions={1} | all-to-all | bytes 2359296 | tf_op jit(solution)/shard_map/all_to_all | solution.py:184
  907.2 3.9 copy.161
  912.4 4.2 fusion.178
  917.6 7.8 fusion.137
  926.4 7.8 fusion.131
  934.9 6.7 fusion.182
  942.3 6.7 fusion.188
  949.0 30.9 %all-gather.20 = bf16[8,1,768]{2,1,0:T(2,128)(2,1)S(1)} all-gather(bf16[1,1,768]{2,1,0:T(2,128)(2,1)} %get-tuple-element.124), channel_id=1, replica_groups=mesh['dp'=8,'seq'=4] {'dp'}, dimensions={0}, use_global_device_ids=true | all-gather | bytes 13824 | tf_op jit(solution)/shard_map/all_gather | solution.py:231
  993.0 3.9 fusion.112
  998.9 13.6 all-reduce.19
  1012.5 31.0 %all-gather.21 = bf16[8,1,4608]{2,1,0:T(2,128)(2,1)S(1)} all-gather(bf16[1,1,4608]{2,1,0:T(2,128)(2,1)S(1)} %bitcast.455), channel_id=1, replica_groups=mesh['dp'=8,'seq'=4] {'dp'}, dimensions={0}, use_global_device_ids=true | all-gather | bytes 82944 | tf_op jit(solution)/shard_map/all_gather | solution.py:275
  1043.6 31.3 %all-gather.22 = bf16[8,1,4608]{2,1,0:T(2,128)(2,1)S(1)} all-gather(bf16[1,1,4608]{2,1,0:T(2,128)(2,1)S(1)} %bitcast.454), channel_id=1, replica_groups=mesh['dp'=8,'seq'=4] {'dp'}, dimensions={0}, use_global_device_ids=true | all-gather | bytes 82944 | tf_op jit(solution)/shard_map/all_gather | solution.py:275
  1075.0 5.0 fusion.100
  1080.1 5.1 fusion.103
  1085.4 38.0 %all-reduce.18 = (f32[1536]{0:T(1024)S(1)}, f32[1536]{0:T(1024)S(1)}, f32[768]{0:T(1024)S(1)}, f32[768]{0:T(1024)S(1)}, f32[3072]{0:T(1024)S(1)}, /*index=5*/f32...) all-reduce(f32[1536]{0:T(1024)S(1)} %copy-done.66, ...), channel_id=25, replica_groups=mesh['dp'=8,'seq'=4] {'dp','seq'}, use_global_device_ids=true, to_apply=%region_43.44.clone | all-reduce | flops 12288 | bytes 98304
  1130.5 89.3 %reduce-scatter.9.cloned.1.call-done = f32[24,2304]{1,0:T(8,128)} async-done(((f32[768,2304]{1,0:T(8,128)}), f32[24,2304]{1,0:T(8,128)}) %reduce-scatter.9.cloned.1.call-update) | async-done | bytes 221200 | tf_op jit(solution)/shard_map/reduce_scatter | solution.py:282
  1221.6 138.7 %reduce-scatter.23.cloned.1.call-done = f32[96,768]{1,0:T(8,128)} async-done(((f32[3072,768]{1,0:T(8,128)}), f32[96,768]{1,0:T(8,128)}) %reduce-scatter.23.cloned.1.call-update) | async-done | bytes 294928 | tf_op jit(solution)/shard_map/reduce_scatter | solution.py:288
  1360.4 141.4 %reduce-scatter.21.cloned.1.call-done = f32[96,768]{1,0:T(8,128)} async-done(((f32[3072,768]{1,0:T(8,128)}), f32[96,768]{1,0:T(8,128)}) %reduce-scatter.21.cloned.1.call-update) | async-done | bytes 294928 | tf_op jit(solution)/shard_map/reduce_scatter | solution.py:288
  1503.7 138.3 %reduce-scatter.19.cloned.1.call-done = f32[24,3072]{1,0:T(8,128)} async-done(((f32[768,3072]{1,0:T(8,128)}), f32[24,3072]{1,0:T(8,128)}) %reduce-scatter.19.cloned.1.call-update) | async-done | bytes 294928 | tf_op jit(solution)/shard_map/reduce_scatter | solution.py:286
  1642.0 141.5 %reduce-scatter.17.cloned.1.call-done = f32[24,3072]{1,0:T(8,128)} async-done(((f32[768,3072]{1,0:T(8,128)}), f32[24,3072]{1,0:T(8,128)}) %reduce-scatter.17.cloned.1.call-update) | async-done | bytes 294928 | tf_op jit(solution)/shard_map/reduce_scatter | solution.py:286
  (510 shorter events, 194.2 us)
Async XLA Ops:
  7.2 13.2 copy-start.122
  7.2 13.7 copy-start.114
  7.2 58.7 %copy-start.4 = (bf16[1,256,768]{2,1,0:T(8,128)(2,1)S(1)}, bf16[1,256,768]{2,1,0:T(8,128)(2,1)}, u32[]{:S(2)}) copy-start(bf16[1,256,768]{2,1,0:T(8,128)(2,1)} %param.13) | copy-start | bytes 1179652
  7.2 59.1 %copy-start.57 = (bf16[1,768]{1,0:T(2,128)(2,1)S(1)}, bf16[1,768]{1,0:T(2,128)(2,1)}, u32[]{:S(2)}) copy-start(bf16[1,768]{1,0:T(2,128)(2,1)} %param.14) | copy-start | bytes 4612
  7.3 79.9 %all-gather.34.cloned.1.call-start = ((), (), s32[]{:S(2)}) async-start(), calls=%async_computation.24 | async-start | bytes 7299072 | tf_op jit(solution)/shard_map/all_gather | solution.py:240
  9.2 152.4 %all-gather.44.cloned.1.call-start = ((), (), s32[]{:S(2)}) async-start(), calls=%async_computation.29 | async-start | bytes 7299072 | tf_op jit(solution)/shard_map/all_gather | solution.py:240
  10.0 213.7 %all-gather.36.cloned.1.call-start = ((), (), s32[]{:S(2)}) async-start(), calls=%async_computation.25 | async-start | bytes 3649536 | tf_op jit(solution)/shard_map/all_gather | solution.py:242
  11.7 273.6 %all-gather.38.cloned.1.call-start = ((), (), s32[]{:S(2)}) async-start(), calls=%async_computation.26 | async-start | bytes 1216512 | tf_op jit(solution)/shard_map/all_gather | solution.py:244
  13.2 332.7 %all-gather.40.cloned.1.call-start = ((), (), s32[]{:S(2)}) async-start(), calls=%async_computation.27 | async-start | bytes 4866048 | tf_op jit(solution)/shard_map/all_gather | solution.py:246
  15.0 396.7 %all-gather.42.cloned.1.call-start = ((), (), s32[]{:S(2)}) async-start(), calls=%async_computation.28 | async-start | bytes 4866048 | tf_op jit(solution)/shard_map/all_gather | solution.py:248
  16.8 456.7 %all-gather.46.cloned.1.call-start = ((), (), s32[]{:S(2)}) async-start(), calls=%async_computation.30 | async-start | bytes 3649536 | tf_op jit(solution)/shard_map/all_gather | solution.py:242
  17.5 530.2 %all-gather.48.cloned.1.call-start = ((), (), s32[]{:S(2)}) async-start(), calls=%async_computation.31 | async-start | bytes 1216512 | tf_op jit(solution)/shard_map/all_gather | solution.py:244
  18.3 577.3 %all-gather.50.cloned.1.call-start = ((), (), s32[]{:S(2)}) async-start(), calls=%async_computation.32 | async-start | bytes 4866048 | tf_op jit(solution)/shard_map/all_gather | solution.py:246
  66.1 157.6 %copy-start.64 = (f32[256]{0:T(256)}, f32[256]{0:T(256)S(1)}, u32[]{:S(2)}) copy-start(f32[256]{0:T(256)S(1)} %broadcast_multiply_fusion.3) | copy-start | bytes 3076
  66.3 20.9 %copy-start.98 = (f32[256]{0:T(256)}, f32[256]{0:T(256)S(1)}, u32[]{:S(2)}) copy-start(f32[256]{0:T(256)S(1)} %fusion.111) | copy-start | bytes 3076
  66.4 157.3 %copy-start.62 = (f32[256]{0:T(256)}, f32[256]{0:T(256)S(1)}, u32[]{:S(2)}) copy-start(f32[256]{0:T(256)S(1)} %fusion.170) | copy-start | bytes 3076
  67.0 94.6 %copy-start.59 = (f32[1,768]{1,0:T(1,128)}, f32[1,768]{1,0:T(1,128)S(1)}, u32[]{:S(2)}) copy-start(f32[1,768]{1,0:T(1,128)S(1)} %get-tuple-element.125) | copy-start | bytes 9220
  166.9 56.8 %copy-start.34 = (f32[768]{0:T(1024)}, f32[768]{0:T(1024)S(1)}, u32[]{:S(2)}) copy-start(f32[768]{0:T(1024)S(1)} %get-tuple-element.88) | copy-start | bytes 9220
  166.9 60.0 %copy-start.47 = (f32[768]{0:T(1024)}, f32[768]{0:T(1024)S(1)}, u32[]{:S(2)}) copy-start(f32[768]{0:T(1024)S(1)} %get-tuple-element.87) | copy-start | bytes 9220
  166.9 179.0 %copy-start.36 = (f32[768]{0:T(1024)}, f32[768]{0:T(1024)S(1)}, u32[]{:S(2)}) copy-start(f32[768]{0:T(1024)S(1)} %get-tuple-element.86) | copy-start | bytes 9220
  166.9 179.0 %copy-start.45 = (f32[768]{0:T(1024)}, f32[768]{0:T(1024)S(1)}, u32[]{:S(2)}) copy-start(f32[768]{0:T(1024)S(1)} %get-tuple-element.85) | copy-start | bytes 9220
  229.7 24.9 %all-to-all-start = ((bf16[1,256,3,768]{1,2,0,3:T(4,128)(2,1)}), bf16[1,256,3,768]{1,2,0,3:T(4,128)(2,1)S(1)}, u32[]{:S(2)}, u32[]{:S(2)}) async-start(bf16[1,256,3,768]{1,2,0,3:T(4,128)(2,1)} %copy.112), calls=%async_computation | async-start | bytes 3145728 | tf_op jit(solution)/shard_map/all_to_all | solution.py:121
  233.2 428.1 %all-gather.52.cloned.1.call-start = ((), (), s32[]{:S(2)}) async-start(), calls=%async_computation.33 | async-start | bytes 4866048 | tf_op jit(solution)/shard_map/all_gather | solution.py:248
  272.5 11.1 all-to-all-start.1
  278.6 194.9 %copy-start.41 = (f32[768]{0:T(1024)}, f32[768]{0:T(1024)S(1)}, u32[]{:S(2)}) copy-start(f32[768]{0:T(1024)S(1)} %get-tuple-element.82) | copy-start | bytes 9220
  278.6 392.1 %copy-start.39 = (f32[768]{0:T(1024)}, f32[768]{0:T(1024)S(1)}, u32[]{:S(2)}) copy-start(f32[768]{0:T(1024)S(1)} %get-tuple-element.80) | copy-start | bytes 9220
  284.9 61.0 %copy-start.93 = (f32[3072]{0:T(1024)S(1)}, f32[3072]{0:T(1024)}, u32[]{:S(2)}) copy-start(f32[3072]{0:T(1024)} %convert_element_type.280) | copy-start | bytes 36868
  285.3 66.2 %copy-start.14 = (bf16[1,256,4,192]{1,3,2,0:T(8,128)(2,1)}, bf16[1,256,4,192]{1,3,2,0:T(8,128)(2,1)S(1)}, u32[]{:S(2)}) copy-start(bf16[1,256,4,192]{1,3,2,0:T(8,128)(2,1)S(1)} %copy.118) | copy-start | bytes 1179652
  288.1 63.3 %copy-start.67 = (f32[256]{0:T(256)}, f32[256]{0:T(256)S(1)}, u32[]{:S(2)}) copy-start(f32[256]{0:T(256)S(1)} %broadcast_multiply_fusion.2) | copy-start | bytes 3076
  288.4 63.1 %copy-start.100 = (f32[256]{0:T(256)}, f32[256]{0:T(256)S(1)}, u32[]{:S(2)}) copy-start(f32[256]{0:T(256)S(1)} %multiply_reduce_fusion.6) | copy-start | bytes 3076
  288.4 63.1 %copy-start.84 = (f32[256]{0:T(256)}, f32[256]{0:T(256)S(1)}, u32[]{:S(2)}) copy-start(f32[256]{0:T(256)S(1)} %fusion.171) | copy-start | bytes 3076
  345.9 65.8 %copy-start.80 = (f32[768]{0:T(1024)S(1)}, f32[768]{0:T(1024)}, u32[]{:S(2)}) copy-start(f32[768]{0:T(1024)} %get-tuple-element.84) | copy-start | bytes 9220
  345.9 65.8 %copy-start.113 = (f32[768]{0:T(1024)S(1)}, f32[768]{0:T(1024)}, u32[]{:S(2)}) copy-start(f32[768]{0:T(1024)} %convert_element_type.281) | copy-start | bytes 9220
  411.7 61.8 %copy-start.51 = (f32[768]{0:T(1024)S(1)}, f32[768]{0:T(1024)}, u32[]{:S(2)}) copy-start(f32[768]{0:T(1024)} %get-tuple-element.81) | copy-start | bytes 9220
  411.7 61.8 %copy-start.94 = (f32[2304]{0:T(1024)S(1)}, f32[2304]{0:T(1024)}, u32[]{:S(2)}) copy-start(f32[2304]{0:T(1024)} %get-tuple-element.158) | copy-start | bytes 27652
  417.9 59.8 %copy-start.72 = (f32[256]{0:T(256)}, f32[256]{0:T(256)S(1)}, u32[]{:S(2)}) copy-start(f32[256]{0:T(256)S(1)} %broadcast_multiply_fusion.1) | copy-start | bytes 3076
  418.1 59.6 %copy-start.102 = (f32[256]{0:T(256)}, f32[256]{0:T(256)S(1)}, u32[]{:S(2)}) copy-start(f32[256]{0:T(256)S(1)} %multiply_reduce_fusion.5) | copy-start | bytes 3076
  418.1 59.6 %copy-start.89 = (f32[256]{0:T(256)}, f32[256]{0:T(256)S(1)}, u32[]{:S(2)}) copy-start(f32[256]{0:T(256)S(1)} %fusion.172) | copy-start | bytes 3076
  530.0 17.7 copy-start.82
  531.4 11.0 all-to-all-start.3
  546.7 48.9 %copy-start.49 = (f32[768]{0:T(1024)S(1)}, f32[768]{0:T(1024)}, u32[]{:S(2)}) copy-start(f32[768]{0:T(1024)} %get-tuple-element.79) | copy-start | bytes 9220
  550.6 120.2 %copy-start.70 = (f32[256]{0:T(256)}, f32[256]{0:T(256)S(1)}, u32[]{:S(2)}) copy-start(f32[256]{0:T(256)S(1)} %broadcast_multiply_fusion) | copy-start | bytes 3076
  595.6 65.8 %copy-start.78 = (f32[768]{0:T(1024)S(1)}, f32[768]{0:T(1024)}, u32[]{:S(2)}) copy-start(f32[768]{0:T(1024)} %get-tuple-element.78) | copy-start | bytes 9220
  688.4 11.8 all-to-all-start.4
  707.8 16.0 slice-start
  754.8 30.2 %all-to-all-start.5 = ((bf16[1,1024,3,192]{3,2,0,1:T(4,128)(2,1)}), bf16[1,1024,3,192]{3,2,0,1:T(4,128)(2,1)}, u32[]{:S(2)}, u32[]{:S(2)}) async-start(bf16[1,1024,3,192]{3,2,0,1:T(4,128)(2,1)} %pad_maximum_fusion), calls=%async_computation.5 | async-start | bytes 4194304 | tf_op jit(solution)/shard_map/all_to_all | solution.py:184
  759.3 369.6 %reduce-scatter.15.cloned.1.call-start = ((), (), s32[]{:S(2)}) async-start(), calls=%async_computation.19 | async-start | bytes 2433024 | tf_op jit(solution)/shard_map/reduce_scatter | solution.py:284
  762.8 28.3 %copy-start.42 = (f32[768]{0:T(1024)S(1)}, f32[768]{0:T(1024)}, u32[]{:S(2)}) copy-start(f32[768]{0:T(1024)} %copy-done.41) | copy-start | bytes 9220
  762.8 28.3 %copy-start.73 = (f32[256]{0:T(256)S(1)}, f32[256]{0:T(256)}, u32[]{:S(2)}) copy-start(f32[256]{0:T(256)} %copy-done.72) | copy-start | bytes 3076
  762.8 28.3 %copy-start.90 = (f32[256]{0:T(256)S(1)}, f32[256]{0:T(256)}, u32[]{:S(2)}) copy-start(f32[256]{0:T(256)} %copy-done.89) | copy-start | bytes 3076
  762.8 366.1 %reduce-scatter.13.cloned.1.call-start = ((), (), s32[]{:S(2)}) async-start(), calls=%async_computation.18 | async-start | bytes 2433024 | tf_op jit(solution)/shard_map/reduce_scatter | solution.py:284
  809.2 321.3 %reduce-scatter.11.cloned.1.call-start = ((), (), s32[]{:S(2)}) async-start(), calls=%async_computation.17 | async-start | bytes 7299072 | tf_op jit(solution)/shard_map/reduce_scatter | solution.py:282
  825.9 12.7 all-to-all-start.6
  830.0 389.8 %reduce-scatter.9.cloned.1.call-start = ((), (), s32[]{:S(2)}) async-start(), calls=%async_computation.16 | async-start | bytes 7299072 | tf_op jit(solution)/shard_map/reduce_scatter | solution.py:282
  916.7 443.7 %reduce-scatter.23.cloned.1.call-start = ((), (), s32[]{:S(2)}) async-start(), calls=%async_computation.23 | async-start | bytes 9732096 | tf_op jit(solution)/shard_map/reduce_scatter | solution.py:288
  925.5 576.3 %reduce-scatter.21.cloned.1.call-start = ((), (), s32[]{:S(2)}) async-start(), calls=%async_computation.22 | async-start | bytes 9732096 | tf_op jit(solution)/shard_map/reduce_scatter | solution.py:288
  934.3 707.8 %reduce-scatter.19.cloned.1.call-start = ((), (), s32[]{:S(2)}) async-start(), calls=%async_computation.21 | async-start | bytes 9732096 | tf_op jit(solution)/shard_map/reduce_scatter | solution.py:286
  941.7 841.9 %reduce-scatter.17.cloned.1.call-start = ((), (), s32[]{:S(2)}) async-start(), calls=%async_computation.20 | async-start | bytes 9732096 | tf_op jit(solution)/shard_map/reduce_scatter | solution.py:286
  949.0 31.7 %copy-start.17 = (f32[256,768]{1,0:T(8,128)S(1)}, f32[256,768]{1,0:T(8,128)}, u32[]{:S(2)}) copy-start(f32[256,768]{1,0:T(8,128)} %copy-done.16) | copy-start | bytes 2359300
  949.0 37.5 %copy-start.6 = (bf16[1,4,256,3,192]{2,1,4,3,0:T(4,128)(2,1)S(1)}, bf16[1,4,256,3,192]{2,1,4,3,0:T(4,128)(2,1)}, u32[]{:S(2)}) copy-start(bf16[1,4,256,3,192]{2,1,4,3,0:T(4,128)(2,1)} %copy.160) | copy-start | bytes 3538948
  949.0 41.1 %copy-start.76 = (f32[768]{0:T(1024)S(1)}, f32[768]{0:T(1024)}, u32[]{:S(2)}) copy-start(f32[768]{0:T(1024)} %get-tuple-element.141) | copy-start | bytes 9220
  1080.1 46.7 %copy-start.77 = (bf16[8,1,24]{2,1,0:T(2,128)(2,1)S(1)}, bf16[8,1,24]{2,1,0:T(2,128)(2,1)}, u32[]{:S(2)}) copy-start(bf16[8,1,24]{2,1,0:T(2,128)(2,1)} %constant_dynamic-slice_fusion) | copy-start | bytes 1156
  1080.1 47.2 %copy-start.58 = (bf16[1,768]{1,0:T(2,128)(2,1)S(1)}, bf16[1,768]{1,0:T(2,128)(2,1)}, u32[]{:S(2)}) copy-start(bf16[1,768]{1,0:T(2,128)(2,1)} %param.14) | copy-start | bytes 4612
  1080.1 47.2 %copy-start.60 = (f32[1,768]{1,0:T(1,128)S(1)}, f32[1,768]{1,0:T(1,128)}, u32[]{:S(2)}) copy-start(f32[1,768]{1,0:T(1,128)} %copy-done.59) | copy-start | bytes 9220
  (92 other events, 415.3 us)
Sparse Core Ops, SparseCore 0:
  11.6 75.5 all-gather.33
  90.7 70.8 all-gather.43
  165.1 58.5 all-gather.35
  227.0 52.9 all-gather.37
  283.3 62.5 all-gather.39
  349.2 62.4 all-gather.41
  414.6 58.8 all-gather.45
  476.4 53.5 all-gather.47
  532.9 62.5 all-gather.49
  598.9 62.4 all-gather.51
  765.4 99.2 reduce-scatter.14
  870.7 98.0 reduce-scatter.12
  974.5 120.4 reduce-scatter.10
  1101.4 118.3 reduce-scatter.8
  1225.5 134.7 reduce-scatter.22
  1367.1 134.6 reduce-scatter.20
  1507.5 134.4 reduce-scatter.18
  1648.8 134.7 reduce-scatter.16
where the time goes:
time: 1800 us; the launch traced here: 1790 us
  waiting for transfers between devices  1150 us (64%)
  blocking collectives  242 us (13%)
  matrix products  179 us (10%)
  local copies, waits for them, and re-layouts  109 us (6%)
  other arithmetic  76.5 us (4%)
  starting transfers between devices  25.3 us (1%)
    reduce_scatter x2, waiting for transfers between devices, on_device(): lax.psum_scatter(grads[6], ('dp', 'seq'), scatter_dimension=0, tiled=True)  280 us
    reduce_scatter x2, waiting for transfers between devices, on_device(): lax.psum_scatter(grads[4], ('dp', 'seq'), scatter_dimension=0, tiled=True)  280 us
    all_gather x2, waiting for transfers between devices, on_device(): lax.all_gather(fc2_weight[layer_at], ('dp', 'seq'), axis=0, tiled=True)  120 us
    all_gather x2, waiting for transfers between devices, on_device(): lax.all_gather(qkv_weight[layer_at], ('dp', 'seq'), axis=0, tiled=True)  112 us
    all_gather x2, waiting for transfers between devices, on_device(): lax.all_gather(fc1_weight[layer_at], ('dp', 'seq'), axis=0, tiled=True)  101 us
    all_gather x2, waiting for transfers between devices, on_device(): lax.all_gather(ada_weight[layer_at], ('dp', 'seq'), axis=0, tiled=True)  90.6 us
    reduce_scatter x2, waiting for transfers between devices, on_device(): lax.psum_scatter(grads[0], ('dp', 'seq'), scatter_dimension=0, tiled=True)  89.3 us
    unnamed x2, blocking collectives  81.8 us
  transfers between devices with their start and end apart: 24, of which 19 were waited for; matrix products, arithmetic and copies ran while one was open for 15% of the time, Pallas kernels for 0%

commit v1 on v0

--- a/solution.py
+++ b/solution.py
@@ -6,6 +6,32 @@
 HD = 64
 
 
+BOTH = ("dp", "seq")
+
+
+def gather_rows(share):
+    return lax.all_gather(share, BOTH, axis=0, tiled=True)
+
+
+def scatter_rows(grad):
+    return lax.psum_scatter(grad, BOTH, scatter_dimension=0, tiled=True)
+
+
+def exchange_rows(grad):
+    groups, members = lax.axis_size("dp"), lax.axis_size("seq")
+    me = lax.axis_index("seq")
+    cut = grad.reshape(groups, members, -1, grad.shape[1])
+    total = lax.dynamic_index_in_dim(cut, me, 1, False)
+    for step in range(1, members):
+        share = lax.dynamic_index_in_dim(cut, me ^ step, 1, False).astype(jnp.bfloat16)
+        came = lax.ppermute(share, "seq", [(at, at ^ step) for at in range(members)])
+        total = total + came.astype(jnp.float32)
+    came = lax.all_to_all(
+        total.astype(jnp.bfloat16), "dp", split_axis=0, concat_axis=0, tiled=True
+    )
+    return jnp.sum(came.astype(jnp.float32), axis=0)
+
+
 epsilon = 1e-06
 
 
@@ -41,14 +67,6 @@
 
 def column_sums(grad):
     return jnp.sum(grad.astype(jnp.float32), axis=(0, 1))
-
-
-def split_mods(params, cond_low):
-    width = params[0].shape[0]
-    mods = jnp.dot(cond_low, params[0], preferred_element_type=jnp.float32) + params[1].astype(
-        jnp.float32
-    )
-    return mods.reshape(mods.shape[0], 6, 1, width)
 
 
 def attention_one(heads):
@@ -108,9 +126,8 @@
     return lax.map(attention_back_one, (heads, log_total, grad_heads))
 
 
-def forward_layer(params, resid, cond_low):
-    qkv_w, qv_b, proj_w, proj_b, fc1_w, fc1_b, fc2_w, fc2_b = params[2:]
-    mods = split_mods(params, cond_low)
+def forward_layer(params, resid, mods):
+    qkv_w, qv_b, proj_w, proj_b, fc1_w, fc1_b, fc2_w, fc2_b = params
     width = resid.shape[2]
     attn_in = (layer_norm(resid) * (1.0 + mods[:, 1]) + mods[:, 0]).astype(jnp.bfloat16)
     query_bias = qv_b[:width].astype(jnp.float32)
@@ -144,7 +161,7 @@
     return (result, kept)
 
 
-def backward_layer(params, kept, grad_new, cond_low):
+def backward_layer(params, kept, grad_new, mods):
     (
         resid,
         attn_in,
@@ -158,8 +175,7 @@
         hidden_act,
         mlp_out,
     ) = kept
-    ada_w, ada_b, qkv_w, qv_b, proj_w, proj_b, fc1_w, fc1_b, fc2_w, fc2_b = params
-    mods = split_mods(params, cond_low)
+    qkv_w, qv_b, proj_w, proj_b, fc1_w, fc1_b, fc2_w, fc2_b = params
     latents, rows, width = resid.shape
     grad_mlp = (grad_new * mods[:, 5]).astype(jnp.bfloat16)
     grad_fc2_w = outer_sum(hidden_act, grad_mlp)
@@ -195,8 +211,6 @@
         [grad_shift_a, grad_scale_a, grad_gate_a, grad_shift_m, grad_scale_m, grad_gate_m], axis=1
     )
     grad_mods = grad_mods.reshape(latents, 6 * width)
-    grad_mods = lax.psum(grad_mods, "seq").astype(jnp.bfloat16)
-    grad_cond = jnp.einsum("bm,dm->bd", grad_mods, ada_w, preferred_element_type=jnp.float32)
     grads = (
         grad_qkv_w,
         grad_qv_b,
@@ -207,7 +221,7 @@
         grad_fc2_w,
         grad_fc2_b,
     )
-    return (grad_resid, grads, grad_cond, grad_mods)
+    return (grad_resid, grads, grad_mods)
 
 
 def on_device(
@@ -226,73 +240,105 @@
     fc2_bias,
 ):
     layers = ada_weight.shape[0]
+    width = conditioning.shape[1]
+    latents = conditioning.shape[0]
+    group = lax.axis_index("dp")
+    owner = lax.axis_index(BOTH)
+    own_rows = ada_weight.shape[1]
     cond_f32 = conditioning.astype(jnp.float32)
     cond_low = jax.nn.silu(cond_f32).astype(jnp.bfloat16)
     cond_every = lax.all_gather(cond_low, "dp", axis=0, tiled=True)
-    owner = lax.axis_index(("dp", "seq"))
-    own_rows = ada_weight.shape[1]
-    own_cols = ada_bias.shape[1]
     cond_rows = lax.dynamic_slice_in_dim(cond_every, owner * own_rows, own_rows, 1)
+    everyone = cond_every.shape[0]
+
+    shares = (ada_bias, qv_bias, proj_bias, fc1_bias, fc2_bias)
+    spread = [
+        lax.dynamic_update_slice_in_dim(
+            jnp.zeros((layers, share.shape[1] * lax.axis_size(BOTH)), jnp.float32),
+            share.astype(jnp.float32),
+            owner * share.shape[1],
+            1,
+        )
+        for share in shares
+    ]
+    partial = jnp.einsum(
+        "bd,ldm->lbm", cond_rows, ada_weight, preferred_element_type=jnp.float32
+    )
+    packed = jnp.concatenate(
+        [partial.reshape(layers, -1)] + spread, axis=1
+    )
+    summed = lax.psum(packed, BOTH)
+    modulated = summed[:, : partial.shape[1] * partial.shape[2]].reshape(partial.shape)
+    at = partial.shape[1] * partial.shape[2]
+    whole = []
+    for one in spread:
+        whole.append(summed[:, at : at + one.shape[1]])
+        at += one.shape[1]
+    mods_own = lax.dynamic_slice_in_dim(modulated, group * latents, latents, 1)
+    mods_own = mods_own + whole[0][:, None]
+
     resid = tokens.astype(jnp.float32)
     kept_all = []
+    params_all = []
+    mods_all = []
     for layer_at in range(layers):
         params = (
-            lax.all_gather(ada_weight[layer_at], ("dp", "seq"), axis=0, tiled=True),
-            lax.all_gather(ada_bias[layer_at], ("dp", "seq"), axis=0, tiled=True),
-            lax.all_gather(qkv_weight[layer_at], ("dp", "seq"), axis=0, tiled=True),
-            lax.all_gather(qv_bias[layer_at], ("dp", "seq"), axis=0, tiled=True),
-            lax.all_gather(proj_weight[layer_at], ("dp", "seq"), axis=0, tiled=True),
-            lax.all_gather(proj_bias[layer_at], ("dp", "seq"), axis=0, tiled=True),
-            lax.all_gather(fc1_weight[layer_at], ("dp", "seq"), axis=0, tiled=True),
-            lax.all_gather(fc1_bias[layer_at], ("dp", "seq"), axis=0, tiled=True),
-            lax.all_gather(fc2_weight[layer_at], ("dp", "seq"), axis=0, tiled=True),
-            lax.all_gather(fc2_bias[layer_at], ("dp", "seq"), axis=0, tiled=True),
+            gather_rows(qkv_weight[layer_at]),
+            whole[1][layer_at],
+            gather_rows(proj_weight[layer_at]),
+            whole[2][layer_at],
+            gather_rows(fc1_weight[layer_at]),
+            whole[3][layer_at],
+            gather_rows(fc2_weight[layer_at]),
+            whole[4][layer_at],
         )
-        resid, kept = forward_layer(params, resid, cond_low)
+        mods = mods_own[layer_at].reshape(latents, 6, 1, width)
+        resid, kept = forward_layer(params, resid, mods)
+        params_all.append(params)
         kept_all.append(kept)
+        mods_all.append(mods)
     grad_resid = cotangent.astype(jnp.float32)
-    grad_cond = jnp.zeros(cond_f32.shape, jnp.float32)
     owned = [None] * layers
-    ada_w_out = [None] * layers
-    ada_b_out = [None] * layers
+    small = [None] * layers
+    mods_sums = [None] * layers
     for layer_at in reversed(range(layers)):
-        params = (
-            lax.all_gather(ada_weight[layer_at], ("dp", "seq"), axis=0, tiled=True),
-            lax.all_gather(ada_bias[layer_at], ("dp", "seq"), axis=0, tiled=True),
-            lax.all_gather(qkv_weight[layer_at], ("dp", "seq"), axis=0, tiled=True),
-            lax.all_gather(qv_bias[layer_at], ("dp", "seq"), axis=0, tiled=True),
-            lax.all_gather(proj_weight[layer_at], ("dp", "seq"), axis=0, tiled=True),
-            lax.all_gather(proj_bias[layer_at], ("dp", "seq"), axis=0, tiled=True),
-            lax.all_gather(fc1_weight[layer_at], ("dp", "seq"), axis=0, tiled=True),
-            lax.all_gather(fc1_bias[layer_at], ("dp", "seq"), axis=0, tiled=True),
-            lax.all_gather(fc2_weight[layer_at], ("dp", "seq"), axis=0, tiled=True),
-            lax.all_gather(fc2_bias[layer_at], ("dp", "seq"), axis=0, tiled=True),
+        grad_resid, grads, mods_sums[layer_at] = backward_layer(
+            params_all[layer_at], kept_all[layer_at], grad_resid, mods_all[layer_at]
         )
-        grad_resid, grads, grad_part, grad_mods = backward_layer(
-            params, kept_all[layer_at], grad_resid, cond_low
+        owned[layer_at] = [exchange_rows(grads[member]) for member in (0, 2, 4)]
+        owned[layer_at].append(scatter_rows(grads[6]))
+        small[layer_at] = jnp.concatenate([grads[member] for member in (1, 3, 5, 7)])
+
+    mods_sum = jnp.stack(mods_sums)
+    mods_spread = lax.dynamic_update_slice_in_dim(
+        jnp.zeros((layers, everyone, mods_sum.shape[2]), jnp.float32), mods_sum, group * latents, 1
+    )
+    total = lax.psum(
+        jnp.concatenate([mods_spread.reshape(layers, -1), jnp.stack(small)], axis=1), BOTH
+    )
+    cut = mods_spread.shape[1] * mods_spread.shape[2]
+    mods_every = total[:, :cut].reshape(mods_spread.shape).astype(jnp.bfloat16)
+    ada_w_grad = jnp.einsum(
+        "bd,lbm->ldm", cond_rows, mods_every, preferred_element_type=jnp.float32
+    )
+    mods_total = jnp.sum(mods_every.astype(jnp.float32), axis=1)
+    ada_b_grad = lax.dynamic_slice_in_dim(
+        mods_total, owner * ada_bias.shape[1], ada_bias.shape[1], 1
+    )
+    bias_grads = []
+    for share in shares[1:]:
+        bias_grads.append(
+            lax.dynamic_slice_in_dim(total, cut + owner * share.shape[1], share.shape[1], 1)
         )
-        grad_cond = grad_cond + grad_part
-        mods_every = lax.all_gather(grad_mods, "dp", axis=0, tiled=True)
-        ada_w_out[layer_at] = jnp.einsum(
-            "bd,bm->dm", cond_rows, mods_every, preferred_element_type=jnp.float32
-        )
-        mods_total = jnp.sum(mods_every.astype(jnp.float32), axis=0)
-        ada_b_out[layer_at] = lax.dynamic_slice_in_dim(mods_total, owner * own_cols, own_cols, 0)
-        owned[layer_at] = (
-            lax.psum_scatter(grads[0], ("dp", "seq"), scatter_dimension=0, tiled=True),
-            lax.psum_scatter(grads[1], ("dp", "seq"), scatter_dimension=0, tiled=True),
-            lax.psum_scatter(grads[2], ("dp", "seq"), scatter_dimension=0, tiled=True),
-            lax.psum_scatter(grads[3], ("dp", "seq"), scatter_dimension=0, tiled=True),
-            lax.psum_scatter(grads[4], ("dp", "seq"), scatter_dimension=0, tiled=True),
-            lax.psum_scatter(grads[5], ("dp", "seq"), scatter_dimension=0, tiled=True),
-            lax.psum_scatter(grads[6], ("dp", "seq"), scatter_dimension=0, tiled=True),
-            lax.psum_scatter(grads[7], ("dp", "seq"), scatter_dimension=0, tiled=True),
-        )
-    results = [
-        jnp.stack([owned[layer_at][member] for layer_at in range(layers)]) for member in range(8)
+        cut += share.shape[1] * lax.axis_size(BOTH)
+    cond_part = jnp.einsum(
+        "lbm,ldm->bd", mods_every, ada_weight, preferred_element_type=jnp.float32
+    )
+    cond_all = lax.all_gather(cond_part, BOTH, axis=1, tiled=True)
+    grad_cond = lax.dynamic_slice_in_dim(cond_all, group * latents, latents, 0)
+    weight_grads = [
+        jnp.stack([owned[layer_at][member] for layer_at in range(layers)]) for member in range(4)
     ]
-    ada_w_grad = jnp.stack(ada_w_out)
-    ada_b_grad = jnp.stack(ada_b_out)
     cond_out = jax.vjp(jax.nn.silu, cond_f32)[1](grad_cond)[0]
     return (
         resid,
@@ -300,14 +346,14 @@
         cond_out,
         ada_w_grad,
         ada_b_grad,
-        results[0],
-        results[1],
-        results[2],
-        results[3],
-        results[4],
-        results[5],
-        results[6],
-        results[7],
+        weight_grads[0],
+        bias_grads[0],
+        weight_grads[1],
+        bias_grads[1],
+        weight_grads[2],
+        bias_grads[2],
+        weight_grads[3],
+        bias_grads[3],
     )
 
 

time: 1800 us -> 1390 us (0.77)
  waiting for transfers between devices: 1150 us -> 791 us
  blocking collectives: 242 us -> 146 us
  starting transfers between devices: 25.3 us -> 68.8 us
  matrix products: 179 us -> 146 us
    reduce_scatter x8 -> x2, waiting for transfers between devices: 649 us -> 80.5 us  [scatter_rows(): return lax.psum_scatter(grad, BOTH, scatter_dimension=0, tiled=True)]
    ppermute x0 -> x18, waiting for transfers between devices: none -> 176 us  [exchange_rows(): lax.ppermute(share, 'seq', [(at, at ^ step) for at in range(members)])]
    psum x0 -> x2, waiting for transfers between devices: none -> 122 us  [the longest x1 122 us: on_device(): summed = lax.psum(packed, BOTH)]
    unnamed x2 -> x0, blocking collectives: 81.8 us -> none
    all_gather x10 -> x8, waiting for transfers between devices: 424 us -> 343 us  [gather_rows(): return lax.all_gather(share, BOTH, axis=0, tiled=True)]
    all_to_all x0 -> x6, starting transfers between devices: none -> 36.8 us  [exchange_rows(): lax.all_to_all(total.astype(jnp.bfloat16), 'dp', split_axis=0, concat_axi...]
    convert_element_type x7 -> x11, other arithmetic: 3.02 us -> 23.2 us  [the longest x6 19.8 us: exchange_rows(): total.astype(jnp.bfloat16)]
    all_gather x2 -> x1, blocking collectives: 62.2 us -> 49.5 us  [on_device(): cond_all = lax.all_gather(cond_part, BOTH, axis=1, tiled=True)]
  transfers between devices with their start and end apart: 24 -> 41, of which waited for: 19 -> 23; matrix products, arithmetic and copies ran while one was open for 15% -> 12% of each run, Pallas kernels for 0% -> 0%
where the time goes in v1:
time: 1390 us; the launch traced here: 1380 us
  waiting for transfers between devices  791 us (57%)
  blocking collectives  146 us (11%)
  matrix products  146 us (11%)
  local copies, waits for them, and re-layouts  123 us (9%)
  other arithmetic  86.9 us (6%)
  starting transfers between devices  68.8 us (5%)
  between operations  16.5 us (1%)
    all_gather x8, waiting for transfers between devices, gather_rows(): return lax.all_gather(share, BOTH, axis=0, tiled=True)  343 us
    ppermute x18, waiting for transfers between devices, exchange_rows(): lax.ppermute(share, 'seq', [(at, at ^ step) for at in range(members)])  176 us
    psum x1, waiting for transfers between devices, on_device(): summed = lax.psum(packed, BOTH)  122 us
    reduce_scatter x2, waiting for transfers between devices, scatter_rows(): return lax.psum_scatter(grad, BOTH, scatter_dimension=0, tiled=True)  80.5 us
    all_gather x1, blocking collectives, on_device(): cond_all = lax.all_gather(cond_part, BOTH, axis=1, tiled=True)  49.5 us
    all_to_all x6, starting transfers between devices, exchange_rows(): lax.all_to_all(total.astype(jnp.bfloat16), 'dp', split_axis=0, concat_axi...  36.8 us
    dot_general x8, matrix products, project(): jnp.einsum('btd,de->bte', left, weight, preferred_element_type=jnp.float32)  35.7 us
    unnamed x176, local copies, waits for them, and re-layouts  34.9 us
  transfers between devices with their start and end apart: 41, of which 23 were waited for; matrix products, arithmetic and copies ran while one was open for 12% of the time, Pallas kernels for 0%

profile of v1, /device:TPU:0, one launch (start us, length us, event | category | flops | bytes accessed | tf_op | source)
XLA Modules:
  0.0 1377.8 jit_solution(16122221219053543068)
XLA Ops:
  12.0 32.1 %all-gather.8 = bf16[8,1,768]{2,1,0:T(2,128)(2,1)S(1)} all-gather(bf16[1,1,768]{2,1,0:T(2,128)(2,1)S(1)} %get-tuple-element.122), channel_id=1, replica_groups=mesh['dp'=8,'seq'=4] {'dp'}, dimensions={0}, use_global_device_ids=true | all-gather | bytes 13824 | tf_op jit(solution)/shard_map/all_gather | solution.py:250
  53.0 121.8 %all-reduce.3.cloned.1.call-done = f32[2,47616]{1,0:T(2,128)} async-done(((f32[2,47616]{1,0:T(2,128)}), f32[2,47616]{1,0:T(2,128)}) %all-reduce.3.cloned.1.call-update) | async-done | bytes 380944 | tf_op jit(solution)/shard_map/psum | solution.py:270
  177.8 60.6 %all-gather.19.cloned.1.call-done = bf16[1,768,2304]{2,1,0:T(8,128)(2,1)} async-done(((bf16[1,24,2304]{2,1,0:T(8,128)(2,1)}), bf16[1,768,2304]{2,1,0:T(8,128)(2,1)}) %all-gather.19.cloned.1.call-update) | async-done | bytes 3538960 | tf_op jit(solution)/shard_map/all_gather | solution.py:13
  248.8 20.6 %all-to-all-done = bf16[1,256,3,768]{1,2,0,3:T(4,128)(2,1)S(1)} async-done(((bf16[1,256,3,768]{1,2,0,3:T(4,128)(2,1)}), bf16[1,256,3,768]{1,2,0,3:T(4,128)(2,1)S(1)}, u32[]{:S(2)}, u32[]{:S(2)}) %all-to-all-start) | async-done | bytes 1179680 | tf_op jit(solution)/shard_map/all_to_all | solution.py:138
  281.8 4.0 reduce.82
  291.9 6.5 all-to-all-done.1
  303.1 57.9 %all-gather.23.cloned.1.call-done = bf16[1,768,3072]{2,1,0:T(8,128)(2,1)} async-done(((bf16[1,24,3072]{2,1,0:T(8,128)(2,1)}), bf16[1,768,3072]{2,1,0:T(8,128)(2,1)}) %all-gather.23.cloned.1.call-update) | async-done | bytes 4718608 | tf_op jit(solution)/shard_map/all_gather | solution.py:13
  361.1 5.5 fusion.26
  366.6 60.7 %all-gather.25.cloned.1.call-done = bf16[1,3072,768]{2,1,0:T(8,128)(2,1)} async-done(((bf16[1,96,768]{2,1,0:T(8,128)(2,1)}), bf16[1,3072,768]{2,1,0:T(8,128)(2,1)}) %all-gather.25.cloned.1.call-update) | async-done | bytes 4718608 | tf_op jit(solution)/shard_map/all_gather | solution.py:13
  427.3 6.1 fusion.197
  433.7 56.3 %all-gather.27.cloned.1.call-done = bf16[1,768,2304]{2,1,0:T(8,128)(2,1)} async-done(((bf16[1,24,2304]{2,1,0:T(8,128)(2,1)}), bf16[1,768,2304]{2,1,0:T(8,128)(2,1)}) %all-gather.27.cloned.1.call-update) | async-done | bytes 3538960 | tf_op jit(solution)/shard_map/all_gather | solution.py:13
  489.9 4.2 fusion.33
  498.8 24.1 %all_to_all.150 = bf16[1,256,3,768]{1,2,0,3:T(4,128)(2,1)S(1)} all-to-all(bf16[1,256,3,768]{1,2,0,3:T(4,128)(2,1)S(1)} %copy.255), channel_id=1, replica_groups=mesh['dp'=8,'seq'=4] {'seq'}, dimensions={3} | all-to-all | bytes 2359296 | tf_op jit(solution)/shard_map/all_to_all | solution.py:138
  541.4 4.9 reduce.83
  547.6 11.0 all_to_all.151
  567.0 46.3 %all-gather.31.cloned.1.call-done = bf16[1,768,3072]{2,1,0:T(8,128)(2,1)} async-done(((bf16[1,24,3072]{2,1,0:T(8,128)(2,1)}), bf16[1,768,3072]{2,1,0:T(8,128)(2,1)}) %all-gather.31.cloned.1.call-update) | async-done | bytes 4718608 | tf_op jit(solution)/shard_map/all_gather | solution.py:13
  613.4 5.4 fusion.29
  618.8 60.9 %all-gather.33.cloned.1.call-done = bf16[1,3072,768]{2,1,0:T(8,128)(2,1)} async-done(((bf16[1,96,768]{2,1,0:T(8,128)(2,1)}), bf16[1,3072,768]{2,1,0:T(8,128)(2,1)}) %all-gather.33.cloned.1.call-update) | async-done | bytes 4718608 | tf_op jit(solution)/shard_map/all_gather | solution.py:13
  679.8 6.4 convert_reduce_fusion
  695.1 4.7 reduce.84
  701.7 4.3 all-to-all-start.4
  706.0 7.5 all-to-all-done.4
  721.1 7.8 fusion.84
  728.9 8.1 multiply_reduce_fusion.1
  737.1 5.3 multiply_convert_fusion.1
  742.4 5.8 fusion.81
  761.8 5.4 pad_maximum_fusion
  767.1 29.3 %all_to_all.152 = bf16[1,1024,3,192]{3,2,0,1:T(4,128)(2,1)} all-to-all(bf16[1,1024,3,192]{3,2,0,1:T(4,128)(2,1)S(1)} %pad_maximum_fusion), channel_id=1, replica_groups=mesh['dp'=8,'seq'=4] {'seq'}, dimensions={1} | all-to-all | bytes 2359296 | tf_op jit(solution)/shard_map/all_to_all | solution.py:200
  796.5 4.3 copy.319
  808.2 5.7 fusion.122
  829.9 7.3 all-to-all-done.6
  838.3 7.7 fusion.87
  846.0 6.4 multiply_reduce_fusion
  853.1 5.3 multiply_convert_fusion
  858.4 5.7 fusion.83
  874.0 6.2 pad_maximum_fusion.1
  880.2 4.6 all-to-all-start.7
  886.3 24.2 %all-to-all-done.7 = bf16[1,1024,3,192]{3,2,0,1:T(4,128)(2,1)} async-done(((bf16[1,1024,3,192]{3,2,0,1:T(4,128)(2,1)}), bf16[1,1024,3,192]{3,2,0,1:T(4,128)(2,1)}, u32[]{:S(2)}, u32[]{:S(2)}) %all-to-all-start.7) | async-done | bytes 1179680 | tf_op jit(solution)/shard_map/all_to_all | solution.py:200
  910.5 3.9 copy.320
  921.6 7.8 fusion.147
  930.4 7.8 fusion.143
  943.7 3.7 copy-done.5
  955.8 54.6 %collective-permute-done.10 = bf16[8,24,768]{2,1,0:T(8,128)(2,1)} collective-permute-done((bf16[8,24,768]{2,1,0:T(8,128)(2,1)S(1)}, bf16[8,24,768]{2,1,0:T(8,128)(2,1)}, u32[]{:S(2)}, u32[]{:S(2)}) %collective-permute-start.10) | collective-permute-done | bytes 294944 | tf_op jit(solution)/shard_map/ppermute | solution.py:27
  1013.6 4.3 all-to-all-start.11
  1019.7 5.7 collective-permute-done.7
  1028.5 4.1 all-to-all-start.10
  1032.6 4.5 fusion.60
  1038.4 5.2 fusion.210
  1043.7 5.9 all-to-all-start.13
  1056.1 3.7 copy-done.6
  1063.9 10.1 collective-permute-done.5
  1074.0 20.1 %collective-permute-done.4 = bf16[8,24,2304]{2,1,0:T(8,128)(2,1)S(1)} collective-permute-done((bf16[8,24,2304]{2,1,0:T(8,128)(2,1)S(1)}, bf16[8,24,2304]{2,1,0:T(8,128)(2,1)S(1)}, u32[]{:S(2)}, u32[]{:S(2)}) %collective-permute-start.4) | collective-permute-done | bytes 884768 | tf_op jit(solution)/shard_map/ppermute | solution.py:27
  1097.0 6.3 all-to-all-start.9
  1104.9 5.2 fusion.209
  1110.1 16.7 %collective-permute-done.14 = bf16[8,24,3072]{2,1,0:T(8,128)(2,1)} collective-permute-done((bf16[8,24,3072]{2,1,0:T(8,128)(2,1)}, bf16[8,24,3072]{2,1,0:T(8,128)(2,1)}, u32[]{:S(2)}, u32[]{:S(2)}) %collective-permute-start.14) | collective-permute-done | bytes 1179680 | tf_op jit(solution)/shard_map/ppermute | solution.py:27
  1126.8 29.0 %collective-permute-done.13 = bf16[8,24,3072]{2,1,0:T(8,128)(2,1)} collective-permute-done((bf16[8,24,3072]{2,1,0:T(8,128)(2,1)}, bf16[8,24,3072]{2,1,0:T(8,128)(2,1)}, u32[]{:S(2)}, u32[]{:S(2)}) %collective-permute-start.13) | collective-permute-done | bytes 1179680 | tf_op jit(solution)/shard_map/ppermute | solution.py:27
  1155.8 4.4 fusion.63
  1160.3 10.7 all-to-all-start.12
  1171.0 4.0 fusion.112
  1182.9 16.4 %collective-permute-done.2 = bf16[8,24,2304]{2,1,0:T(8,128)(2,1)} collective-permute-done((bf16[8,24,2304]{2,1,0:T(8,128)(2,1)}, bf16[8,24,2304]{2,1,0:T(8,128)(2,1)}, u32[]{:S(2)}, u32[]{:S(2)}) %collective-permute-start.2) | collective-permute-done | bytes 884768 | tf_op jit(solution)/shard_map/ppermute | solution.py:27
  1199.3 21.3 %collective-permute-done.1 = bf16[8,24,2304]{2,1,0:T(8,128)(2,1)} collective-permute-done((bf16[8,24,2304]{2,1,0:T(8,128)(2,1)S(1)}, bf16[8,24,2304]{2,1,0:T(8,128)(2,1)}, u32[]{:S(2)}, u32[]{:S(2)}) %collective-permute-start.1) | collective-permute-done | bytes 884768 | tf_op jit(solution)/shard_map/ppermute | solution.py:27
  1224.3 5.5 all-to-all-start.8
  1229.8 49.5 %all-gather.9 = f32[32,24,8]{1,2,0:T(8,128)S(1)} all-gather(f32[1,24,8]{1,2,0:T(8,128)S(1)} %convolution_bitcast_fusion.2), channel_id=1, replica_groups=mesh['dp'=8,'seq'=4] {'dp','seq'}, dimensions={0}, use_global_device_ids=true | all-gather | bytes 25344 | tf_op jit(solution)/shard_map/all_gather | solution.py:337
  1288.1 80.5 %reduce-scatter.3.cloned.1.call-done = f32[96,768]{1,0:T(8,128)} async-done(((f32[3072,768]{1,0:T(8,128)}), f32[96,768]{1,0:T(8,128)}) %reduce-scatter.3.cloned.1.call-update) | async-done | bytes 294928 | tf_op jit(solution)/shard_map/reduce_scatter | solution.py:17
  (438 shorter events, 219.1 us)
Async XLA Ops:
  7.2 37.0 %copy-start = (bf16[2,24,4608]{2,1,0:T(8,128)(2,1)S(1)}, bf16[2,24,4608]{2,1,0:T(8,128)(2,1)}, u32[]{:S(2)}) copy-start(bf16[2,24,4608]{2,1,0:T(8,128)(2,1)} %param.16) | copy-start | bytes 1327108
  7.2 41.0 %copy-start.47 = (bf16[2,24,768]{2,1,0:T(8,128)(2,1)S(1)}, bf16[2,24,768]{2,1,0:T(8,128)(2,1)}, u32[]{:S(2)}) copy-start(bf16[2,24,768]{2,1,0:T(8,128)(2,1)} %param.20) | copy-start | bytes 221188
  7.2 41.7 %copy-start.43 = (bf16[2,24,3072]{2,1,0:T(8,128)(2,1)S(1)}, bf16[2,24,3072]{2,1,0:T(8,128)(2,1)}, u32[]{:S(2)}) copy-start(bf16[2,24,3072]{2,1,0:T(8,128)(2,1)} %param.22) | copy-start | bytes 884740
  7.2 42.5 %copy-start.44 = (bf16[2,96,768]{2,1,0:T(8,128)(2,1)S(1)}, bf16[2,96,768]{2,1,0:T(8,128)(2,1)}, u32[]{:S(2)}) copy-start(bf16[2,96,768]{2,1,0:T(8,128)(2,1)} %param.24) | copy-start | bytes 884740
  7.2 45.4 %copy-start.10 = (bf16[1,256,768]{2,1,0:T(8,128)(2,1)S(1)}, bf16[1,256,768]{2,1,0:T(8,128)(2,1)}, u32[]{:S(2)}) copy-start(bf16[1,256,768]{2,1,0:T(8,128)(2,1)} %param.13) | copy-start | bytes 1179652
  7.2 167.6 %all-reduce.3.cloned.1.call-start = ((), (), s32[]{:S(2)}) async-start(), calls=%async_computation.16 | async-start | bytes 761856 | tf_op jit(solution)/shard_map/psum | solution.py:270
  44.2 131.7 %copy-start.52 = (bf16[8,1,24]{2,1,0:T(2,128)(2,1)}, bf16[8,1,24]{2,1,0:T(2,128)(2,1)S(1)}, u32[]{:S(2)}) copy-start(bf16[8,1,24]{2,1,0:T(2,128)(2,1)S(1)} %constant_dynamic-slice_fusion.6) | copy-start | bytes 1156
  46.4 192.0 %all-gather.19.cloned.1.call-start = ((), (), s32[]{:S(2)}) async-start(), calls=%async_computation.20 | async-start | bytes 3649536 | tf_op jit(solution)/shard_map/all_gather | solution.py:13
  48.1 251.9 %all-gather.21.cloned.1.call-start = ((), (), s32[]{:S(2)}) async-start(), calls=%async_computation.21 | async-start | bytes 1216512 | tf_op jit(solution)/shard_map/all_gather | solution.py:13
  48.9 312.2 %all-gather.23.cloned.1.call-start = ((), (), s32[]{:S(2)}) async-start(), calls=%async_computation.22 | async-start | bytes 4866048 | tf_op jit(solution)/shard_map/all_gather | solution.py:13
  49.7 377.6 %all-gather.25.cloned.1.call-start = ((), (), s32[]{:S(2)}) async-start(), calls=%async_computation.23 | async-start | bytes 4866048 | tf_op jit(solution)/shard_map/all_gather | solution.py:13
  50.5 439.4 %all-gather.27.cloned.1.call-start = ((), (), s32[]{:S(2)}) async-start(), calls=%async_computation.24 | async-start | bytes 3649536 | tf_op jit(solution)/shard_map/all_gather | solution.py:13
  51.1 512.9 %all-gather.29.cloned.1.call-start = ((), (), s32[]{:S(2)}) async-start(), calls=%async_computation.25 | async-start | bytes 1216512 | tf_op jit(solution)/shard_map/all_gather | solution.py:13
  51.8 561.5 %all-gather.31.cloned.1.call-start = ((), (), s32[]{:S(2)}) async-start(), calls=%async_computation.26 | async-start | bytes 4866048 | tf_op jit(solution)/shard_map/all_gather | solution.py:13
  52.7 188.9 %copy-start.56 = (f32[256]{0:T(256)}, f32[256]{0:T(256)S(1)}, u32[]{:S(2)}) copy-start(f32[256]{0:T(256)S(1)} %broadcast_multiply_fusion.3) | copy-start | bytes 3076
  53.0 123.7 %copy-start.60 = (f32[256]{0:T(256)}, f32[256]{0:T(256)S(1)}, u32[]{:S(2)}) copy-start(f32[256]{0:T(256)S(1)} %fusion.119) | copy-start | bytes 3076
  53.0 188.6 %copy-start.50 = (f32[256]{0:T(256)}, f32[256]{0:T(256)S(1)}, u32[]{:S(2)}) copy-start(f32[256]{0:T(256)S(1)} %fusion.179) | copy-start | bytes 3076
  177.8 63.8 %copy-start.48 = (f32[768]{0:T(1024)}, f32[768]{0:T(1024)S(1)}, u32[]{:S(2)}) copy-start(f32[768]{0:T(1024)S(1)} %get-tuple-element.98) | copy-start | bytes 9220
  177.8 63.8 %copy-start.54 = (f32[768]{0:T(1024)}, f32[768]{0:T(1024)S(1)}, u32[]{:S(2)}) copy-start(f32[768]{0:T(1024)S(1)} %get-tuple-element.97) | copy-start | bytes 9220
  244.5 24.9 %all-to-all-start = ((bf16[1,256,3,768]{1,2,0,3:T(4,128)(2,1)}), bf16[1,256,3,768]{1,2,0,3:T(4,128)(2,1)S(1)}, u32[]{:S(2)}, u32[]{:S(2)}) async-start(bf16[1,256,3,768]{1,2,0,3:T(4,128)(2,1)} %copy.247), calls=%async_computation | async-start | bytes 3145728 | tf_op jit(solution)/shard_map/all_to_all | solution.py:138
  248.0 431.7 %all-gather.33.cloned.1.call-start = ((), (), s32[]{:S(2)}) async-start(), calls=%async_computation.27 | async-start | bytes 4866048 | tf_op jit(solution)/shard_map/all_gather | solution.py:13
  287.2 11.1 all-to-all-start.1
  300.0 66.5 %copy-start.20 = (bf16[1,256,4,192]{1,3,2,0:T(8,128)(2,1)}, bf16[1,256,4,192]{1,3,2,0:T(8,128)(2,1)S(1)}, u32[]{:S(2)}) copy-start(bf16[1,256,4,192]{1,3,2,0:T(8,128)(2,1)S(1)} %copy.253) | copy-start | bytes 1179652
  701.7 11.8 all-to-all-start.4
  721.1 16.0 %slice-start.3 = ((s8[12582912]{0:T(1024)(128)(4,1)}), s8[4194304]{0:T(1024)(128)(4,1)S(1)}, s32[]{:S(2)}) async-start(s8[12582912]{0:T(1024)(128)(4,1)} %bitcast.540), calls=%async_computation.31 | async-start | bytes 8388608
  728.9 8.1 slice-start.4
  728.9 8.1 slice-start.5
  806.0 8.1 slice-start.8
  808.2 9.0 slice-start.6
  820.5 17.1 %copy-start.24 = (bf16[1,256,768]{2,1,0:T(8,128)(2,1)}, bf16[1,256,768]{2,1,0:T(8,128)(2,1)S(1)}, u32[]{:S(2)}) copy-start(bf16[1,256,768]{2,1,0:T(8,128)(2,1)S(1)} %get-tuple-element.107) | copy-start | bytes 1179652
  826.2 11.0 all-to-all-start.6
  838.3 14.2 %slice-start = ((s8[12582912]{0:T(1024)(128)(4,1)}), s8[4194304]{0:T(1024)(128)(4,1)S(1)}, s32[]{:S(2)}) async-start(s8[12582912]{0:T(1024)(128)(4,1)} %bitcast.538), calls=%async_computation.28 | async-start | bytes 8388608
  880.2 30.3 %all-to-all-start.7 = ((bf16[1,1024,3,192]{3,2,0,1:T(4,128)(2,1)}), bf16[1,1024,3,192]{3,2,0,1:T(4,128)(2,1)}, u32[]{:S(2)}, u32[]{:S(2)}) async-start(bf16[1,1024,3,192]{3,2,0,1:T(4,128)(2,1)} %pad_maximum_fusion.1), calls=%async_computation.7 | async-start | bytes 4194304 | tf_op jit(solution)/shard_map/all_to_all | solution.py:200
  884.7 294.1 %all-reduce.5.cloned.1.call-start = ((), (), s32[]{:S(2)}) async-start(), calls=%async_computation.17 | async-start | bytes 688128 | tf_op jit(solution)/shard_map/psum | solution.py:316
  921.6 366.5 %reduce-scatter.5.cloned.1.call-start = ((), (), s32[]{:S(2)}) async-start(), calls=%async_computation.19 | async-start | bytes 9732096 | tf_op jit(solution)/shard_map/reduce_scatter | solution.py:17
  929.4 439.1 %reduce-scatter.3.cloned.1.call-start = ((), (), s32[]{:S(2)}) async-start(), calls=%async_computation.18 | async-start | bytes 9732096 | tf_op jit(solution)/shard_map/reduce_scatter | solution.py:17
  940.9 13.3 collective-permute-start.9
  940.9 14.1 %collective-permute-start.11 = (bf16[8,24,768]{2,1,0:T(8,128)(2,1)S(1)}, bf16[8,24,768]{2,1,0:T(8,128)(2,1)S(1)}, u32[]{:S(2)}, u32[]{:S(2)}) collective-permute-start(bf16[8,24,768]{2,1,0:T(8,128)(2,1)S(1)} %get-tuple-element.140), channel_id=1, source_target_pairs={{0,3},{1,2},{2,1},{3,0},{4,7},{5,6},{6,5},{7,4},{8,11},{9,10},{10,... | collective-permute-start | bytes 884744 | tf_op jit(solution)/shard_map/ppermute | solution.py:27
  949.3 83.2 %collective-permute-start.15 = (bf16[8,24,3072]{2,1,0:T(8,128)(2,1)}, bf16[8,24,3072]{2,1,0:T(8,128)(2,1)}, u32[]{:S(2)}, u32[]{:S(2)}) collective-permute-start(bf16[8,24,3072]{2,1,0:T(8,128)(2,1)} %get-tuple-element.127), channel_id=1, source_target_pairs={{0,1},{1,0},{2,3},{3,2},{4,5},{5,4},{6,7},{7,6},{8,9},{9,8},{10,11... | collective-permute-start | bytes 3538952 | tf_op jit(solution)/shard_map/ppermute | solution.py:27
  949.3 83.2 %collective-permute-start.17 = (bf16[8,24,3072]{2,1,0:T(8,128)(2,1)}, bf16[8,24,3072]{2,1,0:T(8,128)(2,1)}, u32[]{:S(2)}, u32[]{:S(2)}) collective-permute-start(bf16[8,24,3072]{2,1,0:T(8,128)(2,1)} %get-tuple-element.128), channel_id=1, source_target_pairs={{0,3},{1,2},{2,1},{3,0},{4,7},{5,6},{6,5},{7,4},{8,11},{9,10},{10,... | collective-permute-start | bytes 3538952 | tf_op jit(solution)/shard_map/ppermute | solution.py:27
  950.3 82.3 %collective-permute-start.16 = (bf16[8,24,3072]{2,1,0:T(8,128)(2,1)}, bf16[8,24,3072]{2,1,0:T(8,128)(2,1)}, u32[]{:S(2)}, u32[]{:S(2)}) collective-permute-start(bf16[8,24,3072]{2,1,0:T(8,128)(2,1)} %get-tuple-element.129), channel_id=1, source_target_pairs={{0,2},{1,3},{2,0},{3,1},{4,6},{5,7},{6,4},{7,5},{8,10},{9,11},{10,... | collective-permute-start | bytes 3538952 | tf_op jit(solution)/shard_map/ppermute | solution.py:27
  954.2 56.1 %collective-permute-start.10 = (bf16[8,24,768]{2,1,0:T(8,128)(2,1)S(1)}, bf16[8,24,768]{2,1,0:T(8,128)(2,1)}, u32[]{:S(2)}, u32[]{:S(2)}) collective-permute-start(bf16[8,24,768]{2,1,0:T(8,128)(2,1)S(1)} %get-tuple-element.141), channel_id=1, source_target_pairs={{0,2},{1,3},{2,0},{3,1},{4,6},{5,7},{6,4},{7,5},{8,10},{9,11},{10,... | collective-permute-start | bytes 884744 | tf_op jit(solution)/shard_map/ppermute | solution.py:27
  955.8 54.6 %collective-permute-start.6 = (bf16[8,24,768]{2,1,0:T(8,128)(2,1)}, bf16[8,24,768]{2,1,0:T(8,128)(2,1)}, u32[]{:S(2)}, u32[]{:S(2)}) collective-permute-start(bf16[8,24,768]{2,1,0:T(8,128)(2,1)} %get-tuple-element.136), channel_id=1, source_target_pairs={{0,1},{1,0},{2,3},{3,2},{4,5},{5,4},{6,7},{7,6},{8,9},{9,8},{10,11... | collective-permute-start | bytes 884744 | tf_op jit(solution)/shard_map/ppermute | solution.py:27
  1010.3 9.3 collective-permute-start.8
  1010.3 15.0 %collective-permute-start.7 = (bf16[8,24,768]{2,1,0:T(8,128)(2,1)S(1)}, bf16[8,24,768]{2,1,0:T(8,128)(2,1)}, u32[]{:S(2)}, u32[]{:S(2)}) collective-permute-start(bf16[8,24,768]{2,1,0:T(8,128)(2,1)S(1)} %get-tuple-element.138), channel_id=1, source_target_pairs={{0,2},{1,3},{2,0},{3,1},{4,6},{5,7},{6,4},{7,5},{8,10},{9,11},{10,... | collective-permute-start | bytes 884744 | tf_op jit(solution)/shard_map/ppermute | solution.py:27
  1013.6 14.9 %all-to-all-start.11 = ((bf16[8,24,768]{2,1,0:T(8,128)(2,1)}), bf16[8,24,768]{2,1,0:T(8,128)(2,1)S(1)}, u32[]{:S(2)}, u32[]{:S(2)}) async-start(bf16[8,24,768]{2,1,0:T(8,128)(2,1)} %fusion.134), calls=%async_computation.11 | async-start | bytes 589824 | tf_op jit(solution)/shard_map/all_to_all | solution.py:29
  1028.5 15.2 %all-to-all-start.10 = ((bf16[8,24,768]{2,1,0:T(8,128)(2,1)}), bf16[8,24,768]{2,1,0:T(8,128)(2,1)}, u32[]{:S(2)}, u32[]{:S(2)}) async-start(bf16[8,24,768]{2,1,0:T(8,128)(2,1)} %fusion.137), calls=%async_computation.10 | async-start | bytes 589824 | tf_op jit(solution)/shard_map/all_to_all | solution.py:29
  1043.7 53.4 %all-to-all-start.13 = ((bf16[8,24,3072]{2,1,0:T(8,128)(2,1)}), bf16[8,24,3072]{2,1,0:T(8,128)(2,1)}, u32[]{:S(2)}, u32[]{:S(2)}) async-start(bf16[8,24,3072]{2,1,0:T(8,128)(2,1)} %fusion.60), calls=%async_computation.13 | async-start | bytes 2359296 | tf_op jit(solution)/shard_map/all_to_all | solution.py:29
  1052.5 10.2 collective-permute-start.3
  1052.6 21.4 %collective-permute-start.5 = (bf16[8,24,2304]{2,1,0:T(8,128)(2,1)S(1)}, bf16[8,24,2304]{2,1,0:T(8,128)(2,1)S(1)}, u32[]{:S(2)}, u32[]{:S(2)}) collective-permute-start(bf16[8,24,2304]{2,1,0:T(8,128)(2,1)S(1)} %get-tuple-element.134), channel_id=1, source_target_pairs={{0,3},{1,2},{2,1},{3,0},{4,7},{5,6},{6,5},{7,4},{8,11},{9,10},{10,... | collective-permute-start | bytes 2654216 | tf_op jit(solution)/shard_map/ppermute | solution.py:27
  1053.4 40.7 %collective-permute-start.4 = (bf16[8,24,2304]{2,1,0:T(8,128)(2,1)S(1)}, bf16[8,24,2304]{2,1,0:T(8,128)(2,1)S(1)}, u32[]{:S(2)}, u32[]{:S(2)}) collective-permute-start(bf16[8,24,2304]{2,1,0:T(8,128)(2,1)S(1)} %get-tuple-element.135), channel_id=1, source_target_pairs={{0,2},{1,3},{2,0},{3,1},{4,6},{5,7},{6,4},{7,5},{8,10},{9,11},{10,... | collective-permute-start | bytes 2654216 | tf_op jit(solution)/shard_map/ppermute | solution.py:27
  1061.8 48.3 %collective-permute-start.12 = (bf16[8,24,3072]{2,1,0:T(8,128)(2,1)}, bf16[8,24,3072]{2,1,0:T(8,128)(2,1)}, u32[]{:S(2)}, u32[]{:S(2)}) collective-permute-start(bf16[8,24,3072]{2,1,0:T(8,128)(2,1)} %get-tuple-element.124), channel_id=1, source_target_pairs={{0,1},{1,0},{2,3},{3,2},{4,5},{5,4},{6,7},{7,6},{8,9},{9,8},{10,11... | collective-permute-start | bytes 3538952 | tf_op jit(solution)/shard_map/ppermute | solution.py:27
  1061.8 65.0 %collective-permute-start.14 = (bf16[8,24,3072]{2,1,0:T(8,128)(2,1)}, bf16[8,24,3072]{2,1,0:T(8,128)(2,1)}, u32[]{:S(2)}, u32[]{:S(2)}) collective-permute-start(bf16[8,24,3072]{2,1,0:T(8,128)(2,1)} %get-tuple-element.125), channel_id=1, source_target_pairs={{0,3},{1,2},{2,1},{3,0},{4,7},{5,6},{6,5},{7,4},{8,11},{9,10},{10,... | collective-permute-start | bytes 3538952 | tf_op jit(solution)/shard_map/ppermute | solution.py:27
  1062.7 40.7 %copy-start.55 = (f32[768]{0:T(1024)S(1)}, f32[768]{0:T(1024)}, u32[]{:S(2)}) copy-start(f32[768]{0:T(1024)} %copy-done.54) | copy-start | bytes 9220
  1062.7 93.2 %collective-permute-start.13 = (bf16[8,24,3072]{2,1,0:T(8,128)(2,1)}, bf16[8,24,3072]{2,1,0:T(8,128)(2,1)}, u32[]{:S(2)}, u32[]{:S(2)}) collective-permute-start(bf16[8,24,3072]{2,1,0:T(8,128)(2,1)} %get-tuple-element.126), channel_id=1, source_target_pairs={{0,2},{1,3},{2,0},{3,1},{4,6},{5,7},{6,4},{7,5},{8,10},{9,11},{10,... | collective-permute-start | bytes 3538952 | tf_op jit(solution)/shard_map/ppermute | solution.py:27
  1097.0 63.2 %all-to-all-start.9 = ((bf16[8,24,2304]{2,1,0:T(8,128)(2,1)}), bf16[8,24,2304]{2,1,0:T(8,128)(2,1)}, u32[]{:S(2)}, u32[]{:S(2)}) async-start(bf16[8,24,2304]{2,1,0:T(8,128)(2,1)} %fusion.66), calls=%async_computation.9 | async-start | bytes 1769472 | tf_op jit(solution)/shard_map/all_to_all | solution.py:29
  1160.3 64.0 %all-to-all-start.12 = ((bf16[8,24,3072]{2,1,0:T(8,128)(2,1)}), bf16[8,24,3072]{2,1,0:T(8,128)(2,1)S(1)}, u32[]{:S(2)}, u32[]{:S(2)}) async-start(bf16[8,24,3072]{2,1,0:T(8,128)(2,1)} %fusion.63), calls=%async_computation.12 | async-start | bytes 2359296 | tf_op jit(solution)/shard_map/all_to_all | solution.py:29
  1175.0 7.9 collective-permute-start
  1175.0 24.4 %collective-permute-start.2 = (bf16[8,24,2304]{2,1,0:T(8,128)(2,1)}, bf16[8,24,2304]{2,1,0:T(8,128)(2,1)}, u32[]{:S(2)}, u32[]{:S(2)}) collective-permute-start(bf16[8,24,2304]{2,1,0:T(8,128)(2,1)} %get-tuple-element.131), channel_id=1, source_target_pairs={{0,3},{1,2},{2,1},{3,0},{4,7},{5,6},{6,5},{7,4},{8,11},{9,10},{10,... | collective-permute-start | bytes 2654216 | tf_op jit(solution)/shard_map/ppermute | solution.py:27
  1175.3 45.3 %collective-permute-start.1 = (bf16[8,24,2304]{2,1,0:T(8,128)(2,1)S(1)}, bf16[8,24,2304]{2,1,0:T(8,128)(2,1)}, u32[]{:S(2)}, u32[]{:S(2)}) collective-permute-start(bf16[8,24,2304]{2,1,0:T(8,128)(2,1)S(1)} %get-tuple-element.132), channel_id=1, source_target_pairs={{0,2},{1,3},{2,0},{3,1},{4,6},{5,7},{6,4},{7,5},{8,10},{9,11},{10,... | collective-permute-start | bytes 2654216 | tf_op jit(solution)/shard_map/ppermute | solution.py:27
  1182.9 98.6 %copy-start.58 = (bf16[1,768]{1,0:T(2,128)(2,1)S(1)}, bf16[1,768]{1,0:T(2,128)(2,1)}, u32[]{:S(2)}) copy-start(bf16[1,768]{1,0:T(2,128)(2,1)} %param.14) | copy-start | bytes 4612
  1182.9 98.6 %copy-start.59 = (f32[1,768]{1,0:T(1,128)S(1)}, f32[1,768]{1,0:T(1,128)}, u32[]{:S(2)}) copy-start(f32[1,768]{1,0:T(1,128)} %get-tuple-element.123) | copy-start | bytes 9220
  1182.9 99.1 %copy-start.53 = (bf16[8,1,24]{2,1,0:T(2,128)(2,1)S(1)}, bf16[8,1,24]{2,1,0:T(2,128)(2,1)}, u32[]{:S(2)}) copy-start(bf16[8,1,24]{2,1,0:T(2,128)(2,1)} %copy-done.52) | copy-start | bytes 1156
  1224.3 62.9 %all-to-all-start.8 = ((bf16[8,24,2304]{2,1,0:T(8,128)(2,1)}), bf16[8,24,2304]{2,1,0:T(8,128)(2,1)S(1)}, u32[]{:S(2)}, u32[]{:S(2)}) async-start(bf16[8,24,2304]{2,1,0:T(8,128)(2,1)} %fusion.69), calls=%async_computation.8 | async-start | bytes 1769472 | tf_op jit(solution)/shard_map/all_to_all | solution.py:29
  (51 other events, 174.2 us)
Sparse Core Ops, SparseCore 0:
  46.5 128.2 all-reduce.2
  178.7 59.6 all-gather.18
  241.8 52.9 all-gather.20
  298.5 62.5 all-gather.22
  364.8 62.4 all-gather.24
  431.0 58.8 all-gather.26
  493.2 53.5 all-gather.28
  550.8 62.5 all-gather.30
  617.3 62.4 all-gather.32
  921.7 126.1 all-reduce.4
  1053.8 173.4 reduce-scatter.4
  1234.1 134.4 reduce-scatter.2
